TPU v7x, 128 devices: a whole 4x4x4 slice. The times are simulated.
128 devices in a mesh: section: 2 (over core), ep: 64 (over y, z, x).
Axes of the slice: x: 4, y: 4, z: 4, core: 2. Of those that a mesh axis runs over, the one named last changes fastest.
Arguments:
- hidden_in: bfloat16 [2, 896, 7168], P(None, ('section', 'ep')), may hold values from -6 to 6
- ffn_gain: float32 [7168], replicated, may hold values from 0.5 to 1.5
- attn_gain: float32 [7168], replicated, may hold values from 0.5 to 1.5
- kv_gain: float32 [512], replicated, may hold values from 0.5 to 1.5
- expert_ids: int32 [2, 896, 4], P(None, ('section', 'ep')), may hold values from 0 to 15, all different within a row; in each aligned block of 7 rows (0 to 6, 7 to 13, ..., all dimensions but the last counted through in order) at most 3 rows name the same one
- route_weight: float32 [2, 896, 4], P(None, ('section', 'ep')), may hold values from 0.05 to 1
- expert_gate: bfloat16 [128, 7168, 256], P(('section', 'ep')), may hold values from -0.0625 to 0.0625
- expert_up: bfloat16 [128, 7168, 256], P(('section', 'ep')), may hold values from -0.0625 to 0.0625
- expert_down: bfloat16 [128, 256, 7168], P(('section', 'ep')), may hold values from -0.125 to 0.125
- kv_down: bfloat16 [7168, 576], P('section'), may hold values from -0.0625 to 0.0625
- resident_cache: bfloat16 [768, 512, 576], P(('section', 'ep')), may hold values from -6 to 6
- fresh_cache: bfloat16 [128, 512, 576], P(('section', 'ep')), may hold values from -6 to 6
- fresh_order: int32 [128], replicated, may hold values from 0 to 127, each once
- cache_len: int32 [896], P(('section', 'ep')), may hold values from 1 to 510, as said below
- queries: bfloat16 [2, 896, 128, 576], P(None, ('section', 'ep')), may hold values from -120 to 120
Outputs:
- layer_out: bfloat16 [2, 896, 7168], P(None, ('section', 'ep'))
- attn_latent: bfloat16 [2, 896, 65536], P(None, ('section', 'ep'))
Inputs may be any that keep to these rules, and one draw needn't show every extreme that they name: `expert_ids`: in each aligned block of 7 rows of one step no expert is named by more than 3 rows, a bound that some block reaches. `fresh_order`: each number once. `cache_len`: some row reaches 510.
All inputs are finite; a program needn't handle non-finite values.
Results may differ from a plain program's by a relative error of at most 0.007.
Values may be sent and summed in bfloat16 or wider, within the bound.
No kernel may reach another device: no remote copies, remote signals or barrier semaphores. Data moves between devices by JAX's collectives and lax.ppermute only.
A program may use at most 192 MiB of HBM per device.

v0:
```python
import functools

import jax
import jax.numpy as jnp
import numpy as np
from jax import lax
from jax.experimental import pallas as pl
from jax.experimental.pallas import tpu as pltpu
from jax.sharding import Mesh, PartitionSpec as P

LAT = 512
ROPE = 64
NOPE = 128
EXPERTS = 16
CAP = 3
BLOCK = 8
META = 128
SIDE = 4
PART = SIDE * CAP
SLOTS = SIDE * PART


epsilon = 1e-06
route_scaling = 2.5
rope_base = 10000.0
masked_score = -1e30
f32 = jnp.float32
bf16 = jnp.bfloat16
NT = (((1,), (1,)), ((), ()))
TN = (((0,), (0,)), ((), ()))


def rms_scale(values, gain_vector):
    values = values.astype(f32)
    return (
        values
        * lax.rsqrt(jnp.mean(values * values, axis=-1, keepdims=True) + epsilon)
        * gain_vector
    )


def shift(values, axis, by):
    size = lax.axis_size(axis)
    return lax.ppermute(values, axis, [(i, (i + by) % size) for i in range(size)])


def add(*terms):
    return sum(term.astype(f32) for term in terms).astype(bf16)


def swap(values):
    return shift(values, "c", 1)


def dot(a, b, dims=(((1,), (0,)), ((), ()))):
    return lax.dot_general(a, b, dims, preferred_element_type=f32)


def call(kernel, outs, *args, smem=0, flops=0, limit=32):
    specs = [pl.BlockSpec(memory_space=pltpu.SMEM)] * smem
    specs += [pl.BlockSpec(memory_space=pltpu.VMEM)] * (len(args) - smem)
    moved = sum(a.size * a.dtype.itemsize for a in args)
    return pl.pallas_call(
        kernel,
        out_shape=[jax.ShapeDtypeStruct(shape, dtype) for shape, dtype in outs],
        in_specs=specs,
        out_specs=[pl.BlockSpec(memory_space=pltpu.VMEM)] * len(outs),
        compiler_params=pltpu.CompilerParams(vmem_limit_bytes=limit * 2**20),
        cost_estimate=pl.CostEstimate(flops=flops, bytes_accessed=moved, transcendentals=0),
    )(*args)


FOLD_ROW = np.arange(SIDE * 2 * PART)
FOLD_BLOCK = FOLD_ROW // (2 * PART)
FOLD_HALF = FOLD_ROW % (2 * PART) // PART
FOLD_SLOT = FOLD_ROW % PART
PLACE = np.stack(
    [
        (np.arange(SLOTS)[:, None] == (FOLD_BLOCK * PART + FOLD_SLOT)[None, :]) & (FOLD_HALF == half)[None, :]
        for half in (0, 1)
    ]
).astype(np.float32)


def fold_tables():
    expert = lax.axis_index("y") * SIDE + (lax.axis_index("z") + FOLD_BLOCK) % SIDE
    lanes = jnp.arange(META)[None, :]
    pick = jnp.stack([expert[:, None] == lanes, expert[:, None] + EXPERTS == lanes]).astype(bf16)
    columns = np.arange(SIDE * BLOCK)
    same = ((FOLD_SLOT // CAP)[:, None] == (columns // BLOCK)[None, :]).astype(np.float32)
    turn = np.broadcast_to((FOLD_SLOT % CAP)[:, None], same.shape).astype(np.float32)
    half = np.broadcast_to(FOLD_HALF[:, None], same.shape).astype(np.float32)
    lower = (columns[None, :] < columns[:, None]) & (
        columns[None, :] // BLOCK == columns[:, None] // BLOCK
    )
    return pick, jnp.asarray(np.stack([same, turn, half])), jnp.asarray(lower.astype(np.float32), bf16)


def select_kernel(pick, fixed, lower, b0, b1, b2, b3, o0, o1, o2, o3, weights):
    held = jnp.concatenate([b[...].astype(f32) for b in (b0, b1, b2, b3)], axis=0)
    width = held.shape[1] - META
    half = width // 2
    meta = held[:, width:]
    lane = lax.broadcasted_iota(jnp.int32, meta.shape, 1)
    named = jnp.where((meta > 0) & (lane < EXPERTS), 1.0, 0.0).astype(bf16)
    meta = meta.astype(bf16)
    before = dot(lower[...], named).astype(bf16)
    here = (dot(pick[0], named, NT) > 0.5) & (dot(pick[0], before, NT) == fixed[1]) & (fixed[0] > 0.5)
    second = fixed[2] > 0.5
    sel = jnp.where(here, 1.0, 0.0)
    low_half = jnp.where(second, 0.0, sel).astype(bf16)
    high_half = jnp.where(second, sel, 0.0).astype(bf16)
    weights[0] = jnp.where(here, dot(pick[0], meta, NT), 0.0)
    weights[1] = jnp.where(here, dot(pick[1], meta, NT), 0.0)
    slots = dot(low_half, held[:, :half].astype(bf16)) + dot(high_half, held[:, half:width].astype(bf16))
    for i, o in enumerate((o0, o1, o2, o3)):
        o[...] = slots[i * 2 * PART : (i + 1) * 2 * PART].astype(bf16)


def assemble_kernel(place, f0, f1, f2, f3, out):
    half = f0.shape[1]
    for h in range(2):
        total = 0.0
        for i, f in enumerate((f0, f1, f2, f3)):
            total = total + dot(place[h, i], f[...])
        out[:, h * half : (h + 1) * half] = total.astype(bf16)


def finish_kernel(place, own, la, ra, lb, rb, o0, o1, o2, o3):
    quarter = la.shape[0]
    half = own.shape[1] // 2
    total = [0.0] * SIDE
    for h in range(2):
        cols = slice(h * half, (h + 1) * half)
        first = own[:quarter, cols].astype(f32) + la[:, cols].astype(f32) + ra[:, cols].astype(f32)
        second = own[quarter:, cols].astype(f32) + lb[:, cols].astype(f32) + rb[:, cols].astype(f32)
        summed = jnp.concatenate([first, second], axis=0).astype(bf16)
        for i in range(SIDE):
            total[i] = total[i] + dot(place[h, i], summed, TN)
    for i, o in enumerate((o0, o1, o2, o3)):
        o[...] = total[i].astype(bf16)


def combine_kernel(fixed, weights, f0, f1, f2, f3, own, o1, o2, o3):
    half = f0.shape[1]
    many = 2 * PART
    for h in range(2):
        cols = slice(h * half, (h + 1) * half)
        total = 0.0
        for i, f in enumerate((f0, f1, f2, f3)):
            rows = slice(i * many, (i + 1) * many)
            mine = (fixed[2, rows] > 0.5) if h else (fixed[2, rows] < 0.5)
            for k in range(2):
                share = jnp.where(mine, weights[k, rows], 0.0).astype(bf16)
                total = total + dot(share, f[...], TN)
        own[:, cols] = total[:BLOCK]
        for i, o in enumerate((o1, o2, o3)):
            o[:, cols] = total[(i + 1) * BLOCK : (i + 2) * BLOCK].astype(bf16)


CHUNK = 512


def expert_kernel(pieces, chunks, *refs):
    xs, others = refs[:pieces], refs[pieces : 2 * pieces]
    gate, up, down, mine, theirs, gate_sum, up_sum, active = refs[2 * pieces :]
    step = pl.program_id(0)

    @pl.when(step == 0)
    def _():
        gate_sum[...] = jnp.zeros_like(gate_sum)
        up_sum[...] = jnp.zeros_like(up_sum)

    @pl.when(step < chunks)
    def _():
        at = 0
        rows = jnp.concatenate([x[...].astype(f32) for x in xs + others], axis=0).astype(bf16)
        gate_sum[...] += dot(rows, gate[0])
        up_sum[...] += dot(rows, up[0])

    @pl.when(step == chunks)
    def _():
        value = gate_sum[...]
        active[...] = (value / (1.0 + jnp.exp(-value)) * up_sum[...]).astype(bf16)

    @pl.when(step >= chunks)
    def _():
        many = mine.shape[0]
        result = dot(active[...], down[0])
        mine[...] = result[:many].astype(bf16)
        theirs[...] = result[many:].astype(bf16)


def experts(xs, others, gate, up, down):
    pieces = len(xs)
    many = sum(x.shape[0] for x in xs)
    width, units = gate.shape[1:]
    chunks = width // CHUNK

    def first(s):
        return jnp.minimum(s, chunks - 1)

    def second(s):
        return jnp.maximum(s - chunks, 0)

    in_specs = [pl.BlockSpec((x.shape[0], CHUNK), lambda s: (0, first(s))) for x in xs + others]
    in_specs += [pl.BlockSpec((1, CHUNK, units), lambda s: (0, first(s), 0))] * 2
    in_specs += [pl.BlockSpec((1, units, CHUNK), lambda s: (0, 0, second(s)))]
    return pl.pallas_call(
        functools.partial(expert_kernel, pieces, chunks),
        grid=(2 * chunks,),
        out_shape=[jax.ShapeDtypeStruct((many, width), bf16)] * 2,
        in_specs=in_specs,
        out_specs=[pl.BlockSpec((many, CHUNK), lambda s: (0, second(s)))] * 2,
        scratch_shapes=[
            pltpu.VMEM((2 * many, units), f32),
            pltpu.VMEM((2 * many, units), f32),
            pltpu.VMEM((2 * many, units), bf16),
        ],
        compiler_params=pltpu.CompilerParams(vmem_limit_bytes=32 * 2**20),
        cost_estimate=pl.CostEstimate(
            flops=12 * many * width * units, bytes_accessed=6 * width * units + 8 * many * width, transcendentals=0
        ),
    )(*xs, *others, gate, up, down)


def past_kernel(scale, lengths, queries, keys, acc, top, total):
    request = pl.program_id(0)
    length = lengths[request]
    held = keys[0]
    steps = queries.shape[0]
    for t in range(steps):
        scores = dot(queries[t, 0], held, TN) * scale
        lane = lax.broadcasted_iota(jnp.int32, scores.shape, 1)
        visible = lane < length
        scores = jnp.where(visible, scores, masked_score)
        highest = jnp.max(scores, axis=-1, keepdims=True)
        weight = jnp.where(visible, jnp.exp(scores - highest), 0.0)
        acc[0, t] = dot(weight.astype(bf16), held[:LAT], NT)
        top[0, t] = highest
        total[0, t] = jnp.sum(weight, axis=-1, keepdims=True)


def past(lengths, queries, keys, scale, start):
    count, width, context = keys.shape
    steps, _, _, heads = queries.shape
    return pl.pallas_call(
        functools.partial(past_kernel, scale),
        grid_spec=pltpu.PrefetchScalarGridSpec(
            num_scalar_prefetch=1,
            grid=(count,),
            in_specs=[
                pl.BlockSpec((steps, 1, width, heads), lambda r, _: (0, r + start, 0, 0)),
                pl.BlockSpec((1, width, context), lambda r, _: (r, 0, 0)),
            ],
            out_specs=[
                pl.BlockSpec((1, steps, heads, LAT), lambda r, _: (r, 0, 0, 0)),
                pl.BlockSpec((1, steps, heads, 1), lambda r, _: (r, 0, 0, 0)),
                pl.BlockSpec((1, steps, heads, 1), lambda r, _: (r, 0, 0, 0)),
            ],
        ),
        out_shape=[
            jax.ShapeDtypeStruct((count, steps, heads, LAT), f32),
            jax.ShapeDtypeStruct((count, steps, heads, 1), f32),
            jax.ShapeDtypeStruct((count, steps, heads, 1), f32),
        ],
        compiler_params=pltpu.CompilerParams(vmem_limit_bytes=32 * 2**20),
        cost_estimate=pl.CostEstimate(
            flops=2 * count * steps * heads * context * (width + LAT),
            bytes_accessed=count * (2 * width * (context + steps * heads) + 4 * steps * heads * LAT),
            transcendentals=count * steps * heads * context,
        ),
    )(lengths, queries, keys)


def merge_kernel(scale, queries, new_keys, acc, top, total, out):
    steps, _, _, heads = queries.shape
    for t in range(steps):
        raw = dot(new_keys[0], queries[t, 0]) * scale
        pad = jnp.zeros((heads - raw.shape[0], heads), f32)
        own = jnp.concatenate([raw, pad], axis=0).T
        highest = top[0, t]
        columns = [own[:, k : k + 1] for k in range(t + 1)]
        peak = highest
        for column in columns:
            peak = jnp.maximum(peak, column)
        keep = jnp.exp(highest - peak)
        weights = [jnp.exp(column - peak) for column in columns]
        below = total[0, t] * keep + sum(weights)
        value = acc[0, t] * (keep / below)
        for k in range(t + 1):
            share = (weights[k] / below).astype(bf16).astype(f32)
            value = value + share * new_keys[0, k : k + 1, :LAT].astype(f32)
        out[0, t] = value.astype(bf16)


def merge(queries, new_keys, acc, top, total, scale, start):
    count, steps, heads, _ = acc.shape
    width = queries.shape[2]
    per = new_keys.shape[1]
    return pl.pallas_call(
        functools.partial(merge_kernel, scale),
        grid=(count,),
        in_specs=[
            pl.BlockSpec((steps, 1, width, heads), lambda r: (0, r + start, 0, 0)),
            pl.BlockSpec((1, per, width), lambda r: (r + start, 0, 0)),
            pl.BlockSpec((1, steps, heads, LAT), lambda r: (r, 0, 0, 0)),
            pl.BlockSpec((1, steps, heads, 1), lambda r: (r, 0, 0, 0)),
            pl.BlockSpec((1, steps, heads, 1), lambda r: (r, 0, 0, 0)),
        ],
        out_specs=pl.BlockSpec((1, steps, heads, LAT), lambda r: (r, 0, 0, 0)),
        out_shape=jax.ShapeDtypeStruct((count, steps, heads, LAT), bf16),
        compiler_params=pltpu.CompilerParams(vmem_limit_bytes=32 * 2**20),
    )(queries, new_keys, acc, top, total)


def project_kernel(core, hidden, own0, a0, b0, c0, own1, a1, b1, c1, gain, kv_own, kv_other, kv_gain, turns, layer, keys):
    rows = []
    for t, (own, a, b, c) in enumerate(((own0, a0, b0, c0), (own1, a1, b1, c1))):
        mixture = own[...] + a[...].astype(f32) + b[...].astype(f32) + c[...].astype(f32)
        rows.append(hidden[t].astype(f32) + mixture)
    both = jnp.concatenate(rows, axis=0).astype(bf16)
    layer[...] = both
    normed = rms_scale(both, gain[...]).astype(bf16)
    half = normed.shape[1] // 2
    swapped = core[0] > 0
    low, high = normed[:, :half].astype(f32), normed[:, half:].astype(f32)
    first = jnp.where(swapped, high, low).astype(bf16)
    second = jnp.where(swapped, low, high).astype(bf16)
    projected = dot(first, kv_own[...], NT) + dot(second, kv_other[...], NT)
    keys[:, :LAT] = rms_scale(projected[:, :LAT], kv_gain[...]).astype(bf16)
    rope = projected[:, LAT:]
    crossed = jnp.concatenate([-rope[:, ROPE // 2 :], rope[:, : ROPE // 2]], axis=1)
    keys[:, LAT:] = (rope * turns[0] + crossed * turns[1]).astype(bf16)


def spread_x(own):
    half = own.shape[0] // 2
    left = shift(own, "x", 1)
    right = shift(own, "x", 3)
    far_a = shift(left[:half], "x", 1)
    far_b = shift(right[half:], "x", 3)
    return [own, left, right, far_a, far_b]


def back_x(place, summed):
    half = SLOTS // 2
    own, left, right, far = [summed[i * SLOTS : (i + 1) * SLOTS] for i in range(SIDE)]
    got_a = shift(far[:half], "x", 1)
    got_b = shift(far[half:], "x", 3)
    from_left_b = shift(right[half:], "x", 1)
    from_right_a = shift(left[:half], "x", 3)
    from_left_a = shift(add(right[:half], got_a), "x", 1)
    from_right_b = shift(add(left[half:], got_b), "x", 3)
    outs = [((2 * PART, own.shape[1] // 2), bf16)] * SIDE
    return call(finish_kernel, outs, place, own, from_left_a, from_right_a, from_left_b, from_right_b)


def fresh_keys(fresh_cache, fresh_order):
    chips = ("y", "z", "x")
    count = lax.axis_size(chips)
    _, width, context = fresh_cache.shape
    tiles = width * context // 1024
    each = -(-tiles // count)

    def to_tiles(array):
        return array.reshape(width // 8, 8, context // 128, 128).swapaxes(1, 2).reshape(tiles, 8, 128)

    def from_tiles(array):
        return array.reshape(width // 8, context // 128, 8, 128).swapaxes(1, 2).reshape(width, context)

    cut = jnp.pad(to_tiles(fresh_cache[0]), ((0, each * count - tiles), (0, 0), (0, 0)))
    cut = cut.reshape(count, each * 8, 128)
    here = lax.all_to_all(cut, chips, split_axis=0, concat_axis=0, tiled=True)
    there = swap(here)
    core = lax.axis_index("c")
    wanted = lax.dynamic_slice_in_dim(fresh_order, core * count, count, 0)
    own_core = (wanted >= count) == (core > 0)
    index = wanted % count
    ordered = jnp.where(own_core[:, None, None], jnp.take(here, index, axis=0), jnp.take(there, index, axis=0))
    whole = lax.all_to_all(ordered, chips, split_axis=0, concat_axis=0, tiled=True)
    return from_tiles(whole.reshape(count * each, 8, 128)[:tiles])[None]


def shards(
    hidden_in,
    ffn_gain,
    attn_gain,
    kv_gain,
    expert_ids,
    route_weight,
    expert_gate,
    expert_up,
    expert_down,
    kv_down,
    resident_cache,
    fresh_cache,
    fresh_order,
    cache_len,
    queries,
):
    steps_count, local_rows, model_width = hidden_in.shape
    resident_rows = resident_cache.shape[0]
    score_scale = (NOPE + ROPE) ** (-0.5)
    core = lax.axis_index("c").astype(jnp.int32).reshape(1)

    shares = route_weight / jnp.sum(route_weight, axis=-1, keepdims=True) * route_scaling
    dense_share = jnp.sum(
        jnp.where(
            expert_ids[..., None] == jnp.arange(EXPERTS, dtype=jnp.int32), shares[..., None], 0.0
        ),
        axis=2,
    )
    high = dense_share.astype(bf16)
    low = (dense_share - high.astype(f32)).astype(bf16)
    normed = rms_scale(hidden_in, ffn_gain).astype(bf16)
    meta_rows = jnp.concatenate(
        [high, low, jnp.zeros((steps_count, local_rows, META - 2 * EXPERTS), bf16)], axis=2
    )
    payload = jnp.pad(
        jnp.concatenate([normed, meta_rows], axis=2), ((0, 0), (0, BLOCK - local_rows), (0, 0))
    )
    hidden_rows = jnp.pad(hidden_in, ((0, 0), (0, BLOCK - local_rows), (0, 0)))

    pick, fixed, lower = fold_tables()
    place = jnp.asarray(
        PLACE.reshape(2, SLOTS, SIDE, 2 * PART).transpose(0, 2, 1, 3), bf16
    )
    folded = ((2 * PART, model_width // 2), bf16)
    query_t = queries.swapaxes(2, 3)
    resident_t = resident_cache.swapaxes(1, 2)

    weights = []
    shared = []
    for step in range(steps_count):
        mine = payload[step]
        held = [mine, shift(mine, "y", 1), shift(mine, "y", 3), shift(mine, "y", 2)]
        *parts, weight = call(
            select_kernel, [folded] * SIDE + [((2, SIDE * 2 * PART, SIDE * BLOCK), f32)],
            pick, fixed, lower, *held,
        )
        weights.append(weight)
        parts = [parts[0], shift(parts[1], "z", 1), shift(parts[2], "z", 2), shift(parts[3], "z", 3)]
        (slots,) = call(assemble_kernel, [((SLOTS, model_width), bf16)], place, *parts)
        shared.append(spread_x(slots))

    fresh_t = fresh_keys(fresh_cache.swapaxes(1, 2), fresh_order)
    other_down = swap(kv_down.T)

    returned = []
    for step in range(steps_count):
        others = [swap(piece) for piece in shared[step]]
        kept, sent = experts(shared[step], others, expert_gate, expert_up, expert_down)
        returned.append(back_x(place, add(kept, swap(sent))))

    past_resident = past(cache_len, query_t, resident_t, score_scale, 0)
    past_fresh = past(cache_len[resident_rows:], query_t, fresh_t, score_scale, resident_rows)

    mixed = []
    for step in range(steps_count):
        parts = returned[step]
        parts = [parts[0], shift(parts[1], "z", 3), shift(parts[2], "z", 2), shift(parts[3], "z", 1)]
        rows = (BLOCK, model_width)
        own, one, two, three = call(
            combine_kernel, [(rows, f32), (rows, bf16), (rows, bf16), (rows, bf16)],
            fixed, weights[step], *parts,
        )
        mixed += [own, shift(one, "y", 3), shift(two, "y", 1), shift(three, "y", 2)]

    positions = jnp.pad(cache_len, (0, BLOCK - local_rows)).astype(f32)[None, :]
    positions = (positions + jnp.arange(steps_count).astype(f32)[:, None]).reshape(-1)
    halfway = ROPE // 2
    frequency = rope_base ** (-2.0 * jnp.arange(halfway).astype(f32) / ROPE)
    angles = positions[:, None] * frequency[None, :]
    turns = jnp.stack([jnp.tile(jnp.cos(angles), (1, 2)), jnp.tile(jnp.sin(angles), (1, 2))])
    many = steps_count * BLOCK
    layer, keys = call(
        project_kernel,
        [((many, model_width), bf16), ((many, LAT + ROPE), bf16)],
        core, hidden_rows, *mixed, attn_gain[None], kv_down.T, other_down, kv_gain[None], turns,
        smem=1, limit=40,
    )
    layer_out = layer.reshape(steps_count, BLOCK, model_width)[:, :local_rows]
    new_keys = jnp.pad(
        keys.reshape(steps_count, BLOCK, LAT + ROPE).swapaxes(0, 1), ((0, 0), (0, BLOCK - steps_count), (0, 0))
    )
    first = merge(query_t, new_keys, *past_resident, score_scale, 0)
    second = merge(query_t, new_keys, *past_fresh, score_scale, resident_rows)
    attended = jnp.concatenate([first, second], axis=0).swapaxes(0, 1)
    return layer_out, attended.reshape(steps_count, local_rows, -1)


def solution(mesh):
    grid = Mesh(mesh.devices.reshape(2, 4, 4, 4), ("c", "y", "z", "x"))
    every = ("c", "y", "z", "x")
    placed = (
        P(None, every, None),
        P(),
        P(),
        P(),
        P(None, every, None),
        P(None, every, None),
        P(every, None, None),
        P(every, None, None),
        P(every, None, None),
        P("c", None),
        P(every, None, None),
        P(every, None, None),
        P(),
        P(every),
        P(None, every, None, None),
    )
    return jax.shard_map(
        shards,
        mesh=grid,
        in_specs=placed,
        out_specs=(P(None, every, None), P(None, every, None)),
        check_vma=False,
    )
```

profile of v0, /device:TPU:0, one launch (start us, length us, event | category | flops | bytes accessed | tf_op | source)
XLA Modules:
  0.0 305.8 jit_solution(15715086880479025102)
XLA Ops:
  12.0 2.8 collective-permute-done.30.b3
  19.7 3.6 %collective-permute-start.32 = (bf16[24,3584]{1,0:T(8,128)(2,1)S(1)}, bf16[24,3584]{1,0:T(8,128)(2,1)S(1)}, u32[]{:S(2)}, u32[]{:S(2)}) collective-permute-start(bf16[24,3584]{1,0:T(8,128)(2,1)S(1)} %get-tuple-element.59), channel_id=1, source_target_pairs={{0,8},{4,12},{8,0},{12,4},{1,9},{5,13},{9,1},{13,5},{2,10},{6,14},... | collective-permute-start | bytes 516104 | tf_op jit(solution)/shard_map/ppermute | solution.py:44
  26.2 4.1 %collective-permute-done.32.f2 = bf16[24,3584]{1,0:T(8,128)(2,1)S(1)} collective-permute-done((bf16[24,3584]{1,0:T(8,128)(2,1)S(1)}, bf16[24,3584]{1,0:T(8,128)(2,1)S(1)}, u32[]{:S(2)}, u32[]{:S(2)}) %collective-permute-start.32) | collective-permute-done | bytes 172064 | tf_op jit(solution)/shard_map/ppermute | solution.py:44
  35.4 13.2 %collective-permute-done.34.refs_1_ = bf16[48,7168]{1,0:T(8,128)(2,1)S(1)} collective-permute-done((bf16[48,7168]{1,0:T(8,128)(2,1)S(1)}, bf16[48,7168]{1,0:T(8,128)(2,1)S(1)}, u32[]{:S(2)}, u32[]{:S(2)}) %collective-permute-start.34) | collective-permute-done | bytes 688160 | tf_op jit(solution)/shard_map/ppermute | solution.py:44
  49.3 2.8 collective-permute-start.37
  52.6 4.6 %collective-permute-done.36.refs_3_ = bf16[24,7168]{1,0:T(8,128)(2,1)S(1)} collective-permute-done((bf16[24,7168]{1,0:T(8,128)(2,1)S(1)}, bf16[24,7168]{1,0:T(8,128)(2,1)S(1)}, u32[]{:S(2)}, u32[]{:S(2)}) %collective-permute-start.36) | collective-permute-done | bytes 344096 | tf_op jit(solution)/shard_map/ppermute | solution.py:44
  65.5 14.7 %shard_map.201 = (bf16[192,7168]{1,0:T(8,128)(2,1)S(1)}, bf16[192,7168]{1,0:T(8,128)(2,1)}) custom-call(bf16[48,7168]{1,0:T(8,128)(2,1)S(1)} %shard_map.200.refs_0_, bf16[48,7168]{1,0:T(8,128)(2,1)S(1)} %collective-permute-done.34.refs_1_, bf16[48,7168]{1,0:T(8,128)(2,1)S(1)} %collective-permute-done.35.refs_2_, ...), custom_call_target="tpu_custom_call" | custom-call | flops 4227858432 | bytes 22020096 | tf_op jit(solution)/shard_map/pallas_call | solution.py:209
  81.2 9.5 %all-to-all-start = ((bf16[64,40,128]{2,1,0:T(8,128)(2,1)}), bf16[64,40,128]{2,1,0:T(8,128)(2,1)}, u32[]{:S(2)}, u32[]{:S(2)}) async-start(bf16[64,40,128]{2,1,0:T(8,128)(2,1)} %bitcast.49), calls=%async_computation | async-start | bytes 1310720 | tf_op jit(solution)/shard_map/all_to_all | solution.py:374
  95.9 8.0 %collective-permute-done.b1 = bf16[8,7296]{1,0:T(8,128)(2,1)S(1)} collective-permute-done((bf16[8,7296]{1,0:T(8,128)(2,1)S(1)}, bf16[8,7296]{1,0:T(8,128)(2,1)S(1)}, u32[]{:S(2)}, u32[]{:S(2)}) %collective-permute-start) | collective-permute-done | bytes 116768 | tf_op jit(solution)/shard_map/ppermute | solution.py:44
  115.5 3.7 %collective-permute-done.4.f2 = bf16[24,3584]{1,0:T(8,128)(2,1)S(1)} collective-permute-done((bf16[24,3584]{1,0:T(8,128)(2,1)S(1)}, bf16[24,3584]{1,0:T(8,128)(2,1)S(1)}, u32[]{:S(2)}, u32[]{:S(2)}) %collective-permute-start.4) | collective-permute-done | bytes 172064 | tf_op jit(solution)/shard_map/ppermute | solution.py:44
  123.9 13.9 %collective-permute-done.6.refs_1_ = bf16[48,7168]{1,0:T(8,128)(2,1)} collective-permute-done((bf16[48,7168]{1,0:T(8,128)(2,1)S(1)}, bf16[48,7168]{1,0:T(8,128)(2,1)}, u32[]{:S(2)}, u32[]{:S(2)}) %collective-permute-start.6) | collective-permute-done | bytes 688160 | tf_op jit(solution)/shard_map/ppermute | solution.py:44
  140.0 3.3 %collective-permute-start.9 = (bf16[24,7168]{1,0:T(8,128)(2,1)S(1)}, bf16[24,7168]{1,0:T(8,128)(2,1)}, u32[]{:S(2)}, u32[]{:S(2)}) collective-permute-start(bf16[24,7168]{1,0:T(8,128)(2,1)S(1)} %slice.115), channel_id=1, source_target_pairs={{0,3},{1,0},{2,1},{3,2},{4,7},{5,4},{6,5},{7,6},{8,11},{9,8},{10,9... | collective-permute-start | bytes 1032200 | tf_op jit(solution)/shard_map/ppermute | solution.py:44
  143.8 4.6 %collective-permute-done.8.refs_3_ = bf16[24,7168]{1,0:T(8,128)(2,1)} collective-permute-done((bf16[24,7168]{1,0:T(8,128)(2,1)S(1)}, bf16[24,7168]{1,0:T(8,128)(2,1)}, u32[]{:S(2)}, u32[]{:S(2)}) %collective-permute-start.8) | collective-permute-done | bytes 344096 | tf_op jit(solution)/shard_map/ppermute | solution.py:44
  161.6 15.9 %shard_map.196 = (bf16[192,7168]{1,0:T(8,128)(2,1)S(1)}, bf16[192,7168]{1,0:T(8,128)(2,1)S(1)}) custom-call(bf16[48,7168]{1,0:T(8,128)(2,1)S(1)} %shard_map.195.refs_0_, bf16[48,7168]{1,0:T(8,128)(2,1)} %collective-permute-done.6.refs_1_, bf16[48,7168]{1,0:T(8,128)(2,1)} %collective-permute-done.7.refs_2_, bf16[24,7168]{1,0:T(8,128)(2,1)} %collective-permute-done.8.refs_3_, ...), custom_call_target="tpu_custom_call" | custom-call | flops 4227858432 | bytes 22020096 | tf_op jit(solution)/shard_map/pallas_call | solution.py:209
  181.6 2.8 collective-permute-start.48
  188.4 4.9 %collective-permute-done.44 = bf16[24,7168]{1,0:T(8,128)(2,1)S(1)} collective-permute-done((bf16[24,7168]{1,0:T(8,128)(2,1)S(1)}, bf16[24,7168]{1,0:T(8,128)(2,1)S(1)}, u32[]{:S(2)}, u32[]{:S(2)}) %collective-permute-start.44) | collective-permute-done | bytes 344096 | tf_op jit(solution)/shard_map/ppermute | solution.py:44
  193.2 3.2 %collective-permute-start.20 = (bf16[24,7168]{1,0:T(8,128)(2,1)S(1)}, bf16[24,7168]{1,0:T(8,128)(2,1)S(1)}, u32[]{:S(2)}, u32[]{:S(2)}) collective-permute-start(bf16[24,7168]{1,0:T(8,128)(2,1)S(1)} %get-tuple-element.93), channel_id=1, source_target_pairs={{0,3},{1,0},{2,1},{3,2},{4,7},{5,4},{6,5},{7,6},{8,11},{9,8},{10,9... | collective-permute-start | bytes 1032200 | tf_op jit(solution)/shard_map/ppermute | solution.py:44
  196.6 3.5 %collective-permute-done.46.ra = bf16[24,7168]{1,0:T(8,128)(2,1)S(1)} collective-permute-done((bf16[24,7168]{1,0:T(8,128)(2,1)S(1)}, bf16[24,7168]{1,0:T(8,128)(2,1)S(1)}, u32[]{:S(2)}, u32[]{:S(2)}) %collective-permute-start.46) | collective-permute-done | bytes 344096 | tf_op jit(solution)/shard_map/ppermute | solution.py:44
  200.2 3.7 %collective-permute-start.18 = (bf16[24,7168]{1,0:T(8,128)(2,1)}, bf16[24,7168]{1,0:T(8,128)(2,1)S(1)}, u32[]{:S(2)}, u32[]{:S(2)}) collective-permute-start(bf16[24,7168]{1,0:T(8,128)(2,1)} %get-tuple-element.95), channel_id=1, source_target_pairs={{0,3},{1,0},{2,1},{3,2},{4,7},{5,4},{6,5},{7,6},{8,11},{9,8},{10,9... | collective-permute-start | bytes 1032200 | tf_op jit(solution)/shard_map/ppermute | solution.py:44
  203.8 4.1 %collective-permute-done.16 = bf16[24,7168]{1,0:T(8,128)(2,1)S(1)} collective-permute-done((bf16[24,7168]{1,0:T(8,128)(2,1)S(1)}, bf16[24,7168]{1,0:T(8,128)(2,1)S(1)}, u32[]{:S(2)}, u32[]{:S(2)}) %collective-permute-start.16) | collective-permute-done | bytes 344096 | tf_op jit(solution)/shard_map/ppermute | solution.py:44
  208.0 3.2 %collective-permute-start.49 = (bf16[24,7168]{1,0:T(8,128)(2,1)S(1)}, bf16[24,7168]{1,0:T(8,128)(2,1)S(1)}, u32[]{:S(2)}, u32[]{:S(2)}) collective-permute-start(bf16[24,7168]{1,0:T(8,128)(2,1)S(1)} %get-tuple-element.85), channel_id=1, source_target_pairs={{0,3},{1,0},{2,1},{3,2},{4,7},{5,4},{6,5},{7,6},{8,11},{9,8},{10,9... | collective-permute-start | bytes 1032200 | tf_op jit(solution)/shard_map/ppermute | solution.py:44
  212.2 10.3 %collective-permute-done.45.la = bf16[24,7168]{1,0:T(8,128)(2,1)S(1)} collective-permute-done((bf16[24,7168]{1,0:T(8,128)(2,1)S(1)}, bf16[24,7168]{1,0:T(8,128)(2,1)S(1)}, u32[]{:S(2)}, u32[]{:S(2)}) %collective-permute-start.45) | collective-permute-done | bytes 344096 | tf_op jit(solution)/shard_map/ppermute | solution.py:44
  222.5 3.2 %collective-permute-start.21 = (bf16[24,7168]{1,0:T(8,128)(2,1)}, bf16[24,7168]{1,0:T(8,128)(2,1)}, u32[]{:S(2)}, u32[]{:S(2)}) collective-permute-start(bf16[24,7168]{1,0:T(8,128)(2,1)} %get-tuple-element.91), channel_id=1, source_target_pairs={{0,3},{1,0},{2,1},{3,2},{4,7},{5,4},{6,5},{7,6},{8,11},{9,8},{10,9... | collective-permute-start | bytes 1032200 | tf_op jit(solution)/shard_map/ppermute | solution.py:44
  226.9 6.5 %all-to-all-start.1 = ((bf16[64,40,128]{2,1,0:T(8,128)(2,1)}), bf16[64,40,128]{2,1,0:T(8,128)(2,1)}, u32[]{:S(2)}, u32[]{:S(2)}) async-start(bf16[64,40,128]{2,1,0:T(8,128)(2,1)} %select_select_fusion), calls=%async_computation.1 | async-start | bytes 1310720 | tf_op jit(solution)/shard_map/all_to_all | solution.py:381
  235.8 2.8 collective-permute-start.50
  249.9 3.6 %collective-permute-start.24 = (bf16[24,3584]{1,0:T(8,128)(2,1)}, bf16[24,3584]{1,0:T(8,128)(2,1)}, u32[]{:S(2)}, u32[]{:S(2)}) collective-permute-start(bf16[24,3584]{1,0:T(8,128)(2,1)} %get-tuple-element.51), channel_id=1, source_target_pairs={{0,4},{4,8},{8,12},{12,0},{1,5},{5,9},{9,13},{13,1},{2,6},{6,10},{... | collective-permute-start | bytes 516104 | tf_op jit(solution)/shard_map/ppermute | solution.py:44
  255.5 2.7 shard_map.203
  262.2 6.8 %shard_map.205 = (f32[6,2,128,512]{3,2,1,0:T(8,128)S(1)}, f32[6,2,128,1]{3,2,1,0:T(8,128)S(1)}, f32[6,2,128,1]{3,2,1,0:T(8,128)S(1)}) custom-call(s32[7]{0:T(128)S(1)} %copy-done.39, bf16[2,7,576,128]{3,2,1,0:T(8,128)(2,1)S(1)} %bitcast.37, bf16[6,576,512]{2,1,0:T(8,128)(2,1)S(1)} %bitcast.48), custom_call_target="tpu_custom_call" | custom-call | flops 1711276032 | bytes 8454144 | tf_op jit(solution)/shard_map/pallas_call | solution.py:247
  272.8 2.9 shard_map.198
  291.3 5.1 %shard_map.204 = (bf16[16,7168]{1,0:T(8,128)(2,1)S(1)}, bf16[16,576]{1,0:T(8,128)(2,1)S(1)}) custom-call(s32[1]{0:T(128)} %bitcast.core, bf16[2,8,7168]{2,1,0:T(8,128)(2,1)S(1)} %pad.20.hidden, f32[8,7168]{1,0:T(8,128)S(1)} %copy-done.20, bf16[8,7168]{1,0:T(8,128)(2,1)} %collective-permute-done.25.a0, bf16[8,7168]{1,0:T(8,128)(2,1)} %collective-permute-done.26.b0, ...), custom_call_target="tpu_custom_call" | custom-call | bytes 9672708 | tf_op jit(solution)/shard_map/pallas_call | solution.py:63
  296.4 4.0 %shard_map.206 = bf16[6,2,128,512]{3,2,1,0:T(8,128)(2,1)S(1)} custom-call(bf16[2,7,576,128]{3,2,1,0:T(8,128)(2,1)S(1)} %bitcast.39, bf16[8,8,576]{2,1,0:T(8,128)(2,1)S(1)} %pad.23.new_keys, f32[6,2,128,512]{3,2,1,0:T(8,128)S(1)} %copy-done.9, f32[6,2,128,1]{3,2,1,0:T(8,128)S(1)} %get-tuple-element.74.top, f32[6,2,128,1]{3,2,1,0:T(8,128)S(1)} %copy-done.16), custom_call_target="tpu_custom_call" | custom-call | tf_op jit(solution)/shard_map/pallas_call | solution.py:301
  301.3 3.6 %reshape.198 = bf16[2,7,65536]{2,0,1:T(2,128)(2,1)} reshape(bf16[2,7,128,512]{3,2,0,1:T(8,128)(2,1)S(1)} %maximum_bitcast_fusion) | data formatting | bytes 3670016 | tf_op jit(solution)/shard_map/reshape | solution.py:490
  (253 shorter events, 123.0 us)
Async XLA Ops:
  32.1 16.5 %collective-permute-start.34 = (bf16[48,7168]{1,0:T(8,128)(2,1)S(1)}, bf16[48,7168]{1,0:T(8,128)(2,1)S(1)}, u32[]{:S(2)}, u32[]{:S(2)}) collective-permute-start(bf16[48,7168]{1,0:T(8,128)(2,1)S(1)} %shard_map.200.refs_0_), channel_id=1, source_target_pairs={{0,1},{1,2},{2,3},{3,0},{4,5},{5,6},{6,7},{7,4},{8,9},{9,10},{10,1... | collective-permute-start | bytes 2064392 | tf_op jit(solution)/shard_map/ppermute | solution.py:44
  33.7 15.6 %collective-permute-start.35 = (bf16[48,7168]{1,0:T(8,128)(2,1)S(1)}, bf16[48,7168]{1,0:T(8,128)(2,1)S(1)}, u32[]{:S(2)}, u32[]{:S(2)}) collective-permute-start(bf16[48,7168]{1,0:T(8,128)(2,1)S(1)} %shard_map.200.refs_0_), channel_id=1, source_target_pairs={{0,3},{1,0},{2,1},{3,2},{4,7},{5,4},{6,5},{7,6},{8,11},{9,8},{10,9... | collective-permute-start | bytes 2064392 | tf_op jit(solution)/shard_map/ppermute | solution.py:44
  35.4 22.3 %collective-permute-start.38 = (bf16[48,7168]{1,0:T(8,128)(2,1)S(1)}, bf16[48,7168]{1,0:T(8,128)(2,1)S(1)}, u32[]{:S(2)}, u32[]{:S(2)}) collective-permute-start(bf16[48,7168]{1,0:T(8,128)(2,1)S(1)} %shard_map.200.refs_0_), channel_id=1, source_target_pairs={{0,64},{64,0},{1,65},{65,1},{2,66},{66,2},{3,67},{67,3},{4,68},{68... | collective-permute-start | bytes 2064392 | tf_op jit(solution)/shard_map/ppermute | solution.py:44
  80.2 97.7 %collective-permute-start.43 = (bf16[192,7168]{1,0:T(8,128)(2,1)}, bf16[192,7168]{1,0:T(8,128)(2,1)}, u32[]{:S(2)}, u32[]{:S(2)}) collective-permute-start(bf16[192,7168]{1,0:T(8,128)(2,1)} %get-tuple-element.62), channel_id=1, source_target_pairs={{0,64},{64,0},{1,65},{65,1},{2,66},{66,2},{3,67},{67,3},{4,68},{68... | collective-permute-start | bytes 8257544 | tf_op jit(solution)/shard_map/ppermute | solution.py:44
  81.2 42.2 %all-to-all-start = ((bf16[64,40,128]{2,1,0:T(8,128)(2,1)}), bf16[64,40,128]{2,1,0:T(8,128)(2,1)}, u32[]{:S(2)}, u32[]{:S(2)}) async-start(bf16[64,40,128]{2,1,0:T(8,128)(2,1)} %bitcast.49), calls=%async_computation | async-start | bytes 1310720 | tf_op jit(solution)/shard_map/all_to_all | solution.py:374
  90.7 13.2 %collective-permute-start = (bf16[8,7296]{1,0:T(8,128)(2,1)S(1)}, bf16[8,7296]{1,0:T(8,128)(2,1)S(1)}, u32[]{:S(2)}, u32[]{:S(2)}) collective-permute-start(bf16[8,7296]{1,0:T(8,128)(2,1)S(1)} %get-tuple-element.98.b0), channel_id=1, source_target_pairs={{0,16},{16,32},{32,48},{48,0},{1,17},{17,33},{33,49},{49,1},{2,18}... | collective-permute-start | bytes 350216 | tf_op jit(solution)/shard_map/ppermute | solution.py:44
  120.1 17.8 %collective-permute-start.6 = (bf16[48,7168]{1,0:T(8,128)(2,1)S(1)}, bf16[48,7168]{1,0:T(8,128)(2,1)}, u32[]{:S(2)}, u32[]{:S(2)}) collective-permute-start(bf16[48,7168]{1,0:T(8,128)(2,1)S(1)} %shard_map.195.refs_0_), channel_id=1, source_target_pairs={{0,1},{1,2},{2,3},{3,0},{4,5},{5,6},{6,7},{7,4},{8,9},{9,10},{10,1... | collective-permute-start | bytes 2064392 | tf_op jit(solution)/shard_map/ppermute | solution.py:44
  121.6 17.3 %collective-permute-start.7 = (bf16[48,7168]{1,0:T(8,128)(2,1)S(1)}, bf16[48,7168]{1,0:T(8,128)(2,1)}, u32[]{:S(2)}, u32[]{:S(2)}) collective-permute-start(bf16[48,7168]{1,0:T(8,128)(2,1)S(1)} %shard_map.195.refs_0_), channel_id=1, source_target_pairs={{0,3},{1,0},{2,1},{3,2},{4,7},{5,4},{6,5},{7,6},{8,11},{9,8},{10,9... | collective-permute-start | bytes 2064392 | tf_op jit(solution)/shard_map/ppermute | solution.py:44
  123.4 19.8 %collective-permute-start.10 = (bf16[48,7168]{1,0:T(8,128)(2,1)S(1)}, bf16[48,7168]{1,0:T(8,128)(2,1)}, u32[]{:S(2)}, u32[]{:S(2)}) collective-permute-start(bf16[48,7168]{1,0:T(8,128)(2,1)S(1)} %shard_map.195.refs_0_), channel_id=1, source_target_pairs={{0,64},{64,0},{1,65},{65,1},{2,66},{66,2},{3,67},{67,3},{4,68},{68... | collective-permute-start | bytes 2064392 | tf_op jit(solution)/shard_map/ppermute | solution.py:44
  123.4 19.8 %collective-permute-start.57 = (bf16[64,40,128]{2,1,0:T(8,128)(2,1)}, bf16[64,40,128]{2,1,0:T(8,128)(2,1)}, u32[]{:S(2)}, u32[]{:S(2)}) collective-permute-start(bf16[64,40,128]{2,1,0:T(8,128)(2,1)} %all-to-all-done), channel_id=1, source_target_pairs={{0,64},{64,0},{1,65},{65,1},{2,66},{66,2},{3,67},{67,3},{4,68},{68... | collective-permute-start | bytes 1966088 | tf_op jit(solution)/shard_map/ppermute | solution.py:44
  143.3 12.2 %collective-permute-start.11 = (bf16[48,7168]{1,0:T(8,128)(2,1)}, bf16[48,7168]{1,0:T(8,128)(2,1)}, u32[]{:S(2)}, u32[]{:S(2)}) collective-permute-start(bf16[48,7168]{1,0:T(8,128)(2,1)} %collective-permute-done.6.refs_1_), channel_id=1, source_target_pairs={{0,64},{64,0},{1,65},{65,1},{2,66},{66,2},{3,67},{67,3},{4,68},{68... | collective-permute-start | bytes 2064392 | tf_op jit(solution)/shard_map/ppermute | solution.py:44
  143.3 12.2 %collective-permute-start.12 = (bf16[48,7168]{1,0:T(8,128)(2,1)}, bf16[48,7168]{1,0:T(8,128)(2,1)}, u32[]{:S(2)}, u32[]{:S(2)}) collective-permute-start(bf16[48,7168]{1,0:T(8,128)(2,1)} %collective-permute-done.7.refs_2_), channel_id=1, source_target_pairs={{0,64},{64,0},{1,65},{65,1},{2,66},{66,2},{3,67},{67,3},{4,68},{68... | collective-permute-start | bytes 2064392 | tf_op jit(solution)/shard_map/ppermute | solution.py:44
  155.3 123.5 %collective-permute-start.56 = (bf16[576,3584]{1,0:T(8,128)(2,1)}, bf16[576,3584]{1,0:T(8,128)(2,1)}, u32[]{:S(2)}, u32[]{:S(2)}) collective-permute-start(bf16[576,3584]{1,0:T(8,128)(2,1)} %bitcast.41), channel_id=1, source_target_pairs={{0,64},{64,0},{1,65},{65,1},{2,66},{66,2},{3,67},{67,3},{4,68},{68... | collective-permute-start | bytes 12386312 | tf_op jit(solution)/shard_map/ppermute | solution.py:44
  180.7 12.5 %collective-permute-start.44 = (bf16[24,7168]{1,0:T(8,128)(2,1)S(1)}, bf16[24,7168]{1,0:T(8,128)(2,1)S(1)}, u32[]{:S(2)}, u32[]{:S(2)}) collective-permute-start(bf16[24,7168]{1,0:T(8,128)(2,1)S(1)} %get-tuple-element.90), channel_id=1, source_target_pairs={{0,1},{1,2},{2,3},{3,0},{4,5},{5,6},{6,7},{7,4},{8,9},{9,10},{10,1... | collective-permute-start | bytes 1032200 | tf_op jit(solution)/shard_map/ppermute | solution.py:44
  184.4 15.7 %collective-permute-start.46 = (bf16[24,7168]{1,0:T(8,128)(2,1)S(1)}, bf16[24,7168]{1,0:T(8,128)(2,1)S(1)}, u32[]{:S(2)}, u32[]{:S(2)}) collective-permute-start(bf16[24,7168]{1,0:T(8,128)(2,1)S(1)} %get-tuple-element.89), channel_id=1, source_target_pairs={{0,3},{1,0},{2,1},{3,2},{4,7},{5,4},{6,5},{7,6},{8,11},{9,8},{10,9... | collective-permute-start | bytes 1032200 | tf_op jit(solution)/shard_map/ppermute | solution.py:44
  186.4 17.5 %collective-permute-start.47 = (bf16[24,7168]{1,0:T(8,128)(2,1)S(1)}, bf16[24,7168]{1,0:T(8,128)(2,1)S(1)}, u32[]{:S(2)}, u32[]{:S(2)}) collective-permute-start(bf16[24,7168]{1,0:T(8,128)(2,1)S(1)} %get-tuple-element.88), channel_id=1, source_target_pairs={{0,1},{1,2},{2,3},{3,0},{4,5},{5,6},{6,7},{7,4},{8,9},{9,10},{10,1... | collective-permute-start | bytes 1032200 | tf_op jit(solution)/shard_map/ppermute | solution.py:44
  193.2 14.7 %collective-permute-start.16 = (bf16[24,7168]{1,0:T(8,128)(2,1)S(1)}, bf16[24,7168]{1,0:T(8,128)(2,1)S(1)}, u32[]{:S(2)}, u32[]{:S(2)}) collective-permute-start(bf16[24,7168]{1,0:T(8,128)(2,1)S(1)} %get-tuple-element.96), channel_id=1, source_target_pairs={{0,1},{1,2},{2,3},{3,0},{4,5},{5,6},{6,7},{7,4},{8,9},{9,10},{10,1... | collective-permute-start | bytes 1032200 | tf_op jit(solution)/shard_map/ppermute | solution.py:44
  193.2 14.7 %collective-permute-start.20 = (bf16[24,7168]{1,0:T(8,128)(2,1)S(1)}, bf16[24,7168]{1,0:T(8,128)(2,1)S(1)}, u32[]{:S(2)}, u32[]{:S(2)}) collective-permute-start(bf16[24,7168]{1,0:T(8,128)(2,1)S(1)} %get-tuple-element.93), channel_id=1, source_target_pairs={{0,3},{1,0},{2,1},{3,2},{4,7},{5,4},{6,5},{7,6},{8,11},{9,8},{10,9... | collective-permute-start | bytes 1032200 | tf_op jit(solution)/shard_map/ppermute | solution.py:44
  200.2 35.6 %collective-permute-start.18 = (bf16[24,7168]{1,0:T(8,128)(2,1)}, bf16[24,7168]{1,0:T(8,128)(2,1)S(1)}, u32[]{:S(2)}, u32[]{:S(2)}) collective-permute-start(bf16[24,7168]{1,0:T(8,128)(2,1)} %get-tuple-element.95), channel_id=1, source_target_pairs={{0,3},{1,0},{2,1},{3,2},{4,7},{5,4},{6,5},{7,6},{8,11},{9,8},{10,9... | collective-permute-start | bytes 1032200 | tf_op jit(solution)/shard_map/ppermute | solution.py:44
  203.8 34.7 %collective-permute-start.19 = (bf16[24,7168]{1,0:T(8,128)(2,1)S(1)}, bf16[24,7168]{1,0:T(8,128)(2,1)S(1)}, u32[]{:S(2)}, u32[]{:S(2)}) collective-permute-start(bf16[24,7168]{1,0:T(8,128)(2,1)S(1)} %get-tuple-element.94), channel_id=1, source_target_pairs={{0,1},{1,2},{2,3},{3,0},{4,5},{5,6},{6,7},{7,4},{8,9},{9,10},{10,1... | collective-permute-start | bytes 1032200 | tf_op jit(solution)/shard_map/ppermute | solution.py:44
  208.0 14.5 %collective-permute-start.45 = (bf16[24,7168]{1,0:T(8,128)(2,1)S(1)}, bf16[24,7168]{1,0:T(8,128)(2,1)S(1)}, u32[]{:S(2)}, u32[]{:S(2)}) collective-permute-start(bf16[24,7168]{1,0:T(8,128)(2,1)S(1)} %get-tuple-element.86), channel_id=1, source_target_pairs={{0,1},{1,2},{2,3},{3,0},{4,5},{5,6},{6,7},{7,4},{8,9},{9,10},{10,1... | collective-permute-start | bytes 1032200 | tf_op jit(solution)/shard_map/ppermute | solution.py:44
  208.0 14.5 %collective-permute-start.49 = (bf16[24,7168]{1,0:T(8,128)(2,1)S(1)}, bf16[24,7168]{1,0:T(8,128)(2,1)S(1)}, u32[]{:S(2)}, u32[]{:S(2)}) collective-permute-start(bf16[24,7168]{1,0:T(8,128)(2,1)S(1)} %get-tuple-element.85), channel_id=1, source_target_pairs={{0,3},{1,0},{2,1},{3,2},{4,7},{5,4},{6,5},{7,6},{8,11},{9,8},{10,9... | collective-permute-start | bytes 1032200 | tf_op jit(solution)/shard_map/ppermute | solution.py:44
  222.5 18.4 %collective-permute-start.17 = (bf16[24,7168]{1,0:T(8,128)(2,1)}, bf16[24,7168]{1,0:T(8,128)(2,1)}, u32[]{:S(2)}, u32[]{:S(2)}) collective-permute-start(bf16[24,7168]{1,0:T(8,128)(2,1)} %get-tuple-element.92), channel_id=1, source_target_pairs={{0,1},{1,2},{2,3},{3,0},{4,5},{5,6},{6,7},{7,4},{8,9},{9,10},{10,1... | collective-permute-start | bytes 1032200 | tf_op jit(solution)/shard_map/ppermute | solution.py:44
  222.5 19.3 %collective-permute-start.21 = (bf16[24,7168]{1,0:T(8,128)(2,1)}, bf16[24,7168]{1,0:T(8,128)(2,1)}, u32[]{:S(2)}, u32[]{:S(2)}) collective-permute-start(bf16[24,7168]{1,0:T(8,128)(2,1)} %get-tuple-element.91), channel_id=1, source_target_pairs={{0,3},{1,0},{2,1},{3,2},{4,7},{5,4},{6,5},{7,6},{8,11},{9,8},{10,9... | collective-permute-start | bytes 1032200 | tf_op jit(solution)/shard_map/ppermute | solution.py:44
  226.9 54.5 %all-to-all-start.1 = ((bf16[64,40,128]{2,1,0:T(8,128)(2,1)}), bf16[64,40,128]{2,1,0:T(8,128)(2,1)}, u32[]{:S(2)}, u32[]{:S(2)}) async-start(bf16[64,40,128]{2,1,0:T(8,128)(2,1)} %select_select_fusion), calls=%async_computation.1 | async-start | bytes 1310720 | tf_op jit(solution)/shard_map/all_to_all | solution.py:381
  240.9 13.6 %collective-permute-start.52 = (bf16[24,3584]{1,0:T(8,128)(2,1)}, bf16[24,3584]{1,0:T(8,128)(2,1)}, u32[]{:S(2)}, u32[]{:S(2)}) collective-permute-start(bf16[24,3584]{1,0:T(8,128)(2,1)} %copy-done.38), channel_id=1, source_target_pairs={{0,4},{4,8},{8,12},{12,0},{1,5},{5,9},{9,13},{13,1},{2,6},{6,10},{... | collective-permute-start | bytes 516104 | tf_op jit(solution)/shard_map/ppermute | solution.py:44
  245.0 25.7 %collective-permute-start.22 = (bf16[24,3584]{1,0:T(8,128)(2,1)}, bf16[24,3584]{1,0:T(8,128)(2,1)}, u32[]{:S(2)}, u32[]{:S(2)}) collective-permute-start(bf16[24,3584]{1,0:T(8,128)(2,1)} %get-tuple-element.49), channel_id=1, source_target_pairs={{0,12},{4,0},{8,4},{12,8},{1,13},{5,1},{9,5},{13,9},{2,14},{6,2},{... | collective-permute-start | bytes 516104 | tf_op jit(solution)/shard_map/ppermute | solution.py:44
  247.6 24.0 %collective-permute-start.23 = (bf16[24,3584]{1,0:T(8,128)(2,1)}, bf16[24,3584]{1,0:T(8,128)(2,1)}, u32[]{:S(2)}, u32[]{:S(2)}) collective-permute-start(bf16[24,3584]{1,0:T(8,128)(2,1)} %get-tuple-element.50), channel_id=1, source_target_pairs={{0,8},{4,12},{8,0},{12,4},{1,9},{5,13},{9,1},{13,5},{2,10},{6,14},... | collective-permute-start | bytes 516104 | tf_op jit(solution)/shard_map/ppermute | solution.py:44
  249.9 22.8 %collective-permute-start.24 = (bf16[24,3584]{1,0:T(8,128)(2,1)}, bf16[24,3584]{1,0:T(8,128)(2,1)}, u32[]{:S(2)}, u32[]{:S(2)}) collective-permute-start(bf16[24,3584]{1,0:T(8,128)(2,1)} %get-tuple-element.51), channel_id=1, source_target_pairs={{0,4},{4,8},{8,12},{12,0},{1,5},{5,9},{9,13},{13,1},{2,6},{6,10},{... | collective-permute-start | bytes 516104 | tf_op jit(solution)/shard_map/ppermute | solution.py:44
  258.9 19.9 %collective-permute-start.53 = (bf16[8,7168]{1,0:T(8,128)(2,1)S(1)}, bf16[8,7168]{1,0:T(8,128)(2,1)S(1)}, u32[]{:S(2)}, u32[]{:S(2)}) collective-permute-start(bf16[8,7168]{1,0:T(8,128)(2,1)S(1)} %get-tuple-element.68), channel_id=1, source_target_pairs={{0,48},{16,0},{32,16},{48,32},{1,49},{17,1},{33,17},{49,33},{2,50}... | collective-permute-start | bytes 344072 | tf_op jit(solution)/shard_map/ppermute | solution.py:44
  270.7 13.5 %collective-permute-start.54 = (bf16[8,7168]{1,0:T(8,128)(2,1)}, bf16[8,7168]{1,0:T(8,128)(2,1)S(1)}, u32[]{:S(2)}, u32[]{:S(2)}) collective-permute-start(bf16[8,7168]{1,0:T(8,128)(2,1)} %get-tuple-element.69), channel_id=1, source_target_pairs={{0,16},{16,32},{32,48},{48,0},{1,17},{17,33},{33,49},{49,1},{2,18}... | collective-permute-start | bytes 344072 | tf_op jit(solution)/shard_map/ppermute | solution.py:44
  271.6 13.3 %collective-permute-start.55 = (bf16[8,7168]{1,0:T(8,128)(2,1)}, bf16[8,7168]{1,0:T(8,128)(2,1)S(1)}, u32[]{:S(2)}, u32[]{:S(2)}) collective-permute-start(bf16[8,7168]{1,0:T(8,128)(2,1)} %get-tuple-element.70), channel_id=1, source_target_pairs={{0,32},{16,48},{32,0},{48,16},{1,33},{17,49},{33,1},{49,17},{2,34}... | collective-permute-start | bytes 344072 | tf_op jit(solution)/shard_map/ppermute | solution.py:44
  (77 other events, 884.4 us)
where the time goes:
time: 308 us; the launch traced here: 306 us
  starting transfers between devices  94.7 us (31%)
  waiting for transfers between devices  88.3 us (29%)
  Pallas kernels  61.5 us (20%)
  local copies, waits for them, and re-layouts  48.8 us (16%)
  other arithmetic  11.3 us (4%)
    ppermute x58, waiting for transfers between devices, shift(): lax.ppermute(values, axis, [(i, (i + by) % size) for i in range(size)])  88.3 us
    ppermute x58, starting transfers between devices, shift(): lax.ppermute(values, axis, [(i, (i + by) % size) for i in range(size)])  78.8 us
    unnamed x101, local copies, waits for them, and re-layouts  31.2 us
    pallas_call x2, Pallas kernels, experts(): pl.pallas_call(functools.partial(expert_kernel, pieces, chunks), grid=(2...  30.6 us
    pallas_call x9, Pallas kernels, call(): pl.pallas_call(kernel, out_shape=[jax.ShapeDtypeStruct(shape, dtype) for...  17.7 us
    all_to_all x1, starting transfers between devices, fresh_keys(): here = lax.all_to_all(cut, chips, split_axis=0, concat_axis=0, tiled=True)  9.46 us
    pallas_call x2, Pallas kernels, past(): pl.pallas_call(functools.partial(past_kernel, scale), grid_spec=pltpu.Pre...  8.51 us
    all_to_all x1, starting transfers between devices, fresh_keys(): lax.all_to_all(ordered, chips, split_axis=0, concat_axis=0, tiled=True)  6.46 us
  transfers between devices with their start and end apart: 60, of which 22 were waited for; matrix products, arithmetic and copies ran while one was open for 7% of the time, Pallas kernels for 12%

commit v1 on v0

--- a/solution.py
+++ b/solution.py
@@ -56,7 +56,7 @@
     return lax.dot_general(a, b, dims, preferred_element_type=f32)
 
 
-def call(kernel, outs, *args, smem=0, flops=0, limit=32):
+def call(kernel, outs, *args, smem=0, flops=0, limit=32, scratch=()):
     specs = [pl.BlockSpec(memory_space=pltpu.SMEM)] * smem
     specs += [pl.BlockSpec(memory_space=pltpu.VMEM)] * (len(args) - smem)
     moved = sum(a.size * a.dtype.itemsize for a in args)
@@ -65,6 +65,7 @@
         out_shape=[jax.ShapeDtypeStruct(shape, dtype) for shape, dtype in outs],
         in_specs=specs,
         out_specs=[pl.BlockSpec(memory_space=pltpu.VMEM)] * len(outs),
+        scratch_shapes=list(scratch),
         compiler_params=pltpu.CompilerParams(vmem_limit_bytes=limit * 2**20),
         cost_estimate=pl.CostEstimate(flops=flops, bytes_accessed=moved, transcendentals=0),
     )(*args)
@@ -126,19 +127,46 @@
         out[:, h * half : (h + 1) * half] = total.astype(bf16)
 
 
-def finish_kernel(place, own, la, ra, lb, rb, o0, o1, o2, o3):
+def finish_kernel(place, own, plus, minus, la, rb, o0, o1, o2, o3):
     quarter = la.shape[0]
     half = own.shape[1] // 2
     total = [0.0] * SIDE
     for h in range(2):
         cols = slice(h * half, (h + 1) * half)
-        first = own[:quarter, cols].astype(f32) + la[:, cols].astype(f32) + ra[:, cols].astype(f32)
-        second = own[quarter:, cols].astype(f32) + lb[:, cols].astype(f32) + rb[:, cols].astype(f32)
+        mine = own[:, cols].astype(f32)
+        first = mine[:quarter] + la[:, cols].astype(f32) + minus[:, cols].astype(f32)[:quarter]
+        second = mine[quarter:] + plus[:, cols].astype(f32)[:quarter] + rb[:, cols].astype(f32)
         summed = jnp.concatenate([first, second], axis=0).astype(bf16)
         for i in range(SIDE):
             total[i] = total[i] + dot(place[h, i], summed, TN)
     for i, o in enumerate((o0, o1, o2, o3)):
         o[...] = total[i].astype(bf16)
+
+
+def pair_kernel(kept, got, own, lb, ra, plus, minus):
+    total = kept[...].astype(f32) + got[...].astype(f32)
+    quarter = lb.shape[0]
+    piece = [total[i * quarter : (i + 1) * quarter] for i in range(8)]
+    own[...] = total[: 2 * quarter].astype(bf16)
+    lb[...] = piece[2].astype(bf16)
+    ra[...] = piece[3].astype(bf16)
+    plus[...] = jnp.concatenate([piece[4], piece[6]], axis=0).astype(bf16)
+    minus[...] = jnp.concatenate([piece[5], piece[7]], axis=0).astype(bf16)
+
+
+def pair_sums(kept, got):
+    many, width = kept.shape
+    rows = (many // 4, many // 8, many // 8, many // 4, many // 4)
+    chunk = 1024
+    return pl.pallas_call(
+        pair_kernel,
+        grid=(width // chunk,),
+        out_shape=[jax.ShapeDtypeStruct((r, width), bf16) for r in rows],
+        in_specs=[pl.BlockSpec((many, chunk), lambda s: (0, s))] * 2,
+        out_specs=[pl.BlockSpec((r, chunk), lambda s: (0, s)) for r in rows],
+        compiler_params=pltpu.CompilerParams(vmem_limit_bytes=24 * 2**20),
+        cost_estimate=pl.CostEstimate(flops=many * width, bytes_accessed=6 * many * width, transcendentals=0),
+    )(kept, got)
 
 
 def combine_kernel(fixed, weights, f0, f1, f2, f3, own, o1, o2, o3):
@@ -158,12 +186,12 @@
             o[:, cols] = total[(i + 1) * BLOCK : (i + 2) * BLOCK].astype(bf16)
 
 
-CHUNK = 512
+CHUNK = 1024
 
 
 def expert_kernel(pieces, chunks, *refs):
     xs, others = refs[:pieces], refs[pieces : 2 * pieces]
-    gate, up, down, mine, theirs, gate_sum, up_sum, active = refs[2 * pieces :]
+    gate, up, down, mine, theirs, rows, gate_sum, up_sum, active = refs[2 * pieces :]
     step = pl.program_id(0)
 
     @pl.when(step == 0)
@@ -174,9 +202,11 @@
     @pl.when(step < chunks)
     def _():
         at = 0
-        rows = jnp.concatenate([x[...].astype(f32) for x in xs + others], axis=0).astype(bf16)
-        gate_sum[...] += dot(rows, gate[0])
-        up_sum[...] += dot(rows, up[0])
+        for x in xs + others:
+            rows[at : at + x.shape[0]] = x[...]
+            at += x.shape[0]
+        gate_sum[...] += dot(rows[...], gate[0])
+        up_sum[...] += dot(rows[...], up[0])
 
     @pl.when(step == chunks)
     def _():
@@ -213,6 +243,7 @@
         in_specs=in_specs,
         out_specs=[pl.BlockSpec((many, CHUNK), lambda s: (0, second(s)))] * 2,
         scratch_shapes=[
+            pltpu.VMEM((2 * many, CHUNK), bf16),
             pltpu.VMEM((2 * many, units), f32),
             pltpu.VMEM((2 * many, units), f32),
             pltpu.VMEM((2 * many, units), bf16),
@@ -273,113 +304,148 @@
     )(lengths, queries, keys)
 
 
-def merge_kernel(scale, queries, new_keys, acc, top, total, out):
+def merge_kernel(scale, count, queries, new_keys, acc, top, total, last_acc, last_top, last_total, out, rows):
     steps, _, _, heads = queries.shape
-    for t in range(steps):
-        raw = dot(new_keys[0], queries[t, 0]) * scale
-        pad = jnp.zeros((heads - raw.shape[0], heads), f32)
-        own = jnp.concatenate([raw, pad], axis=0).T
-        highest = top[0, t]
-        columns = [own[:, k : k + 1] for k in range(t + 1)]
-        peak = highest
-        for column in columns:
-            peak = jnp.maximum(peak, column)
-        keep = jnp.exp(highest - peak)
-        weights = [jnp.exp(column - peak) for column in columns]
-        below = total[0, t] * keep + sum(weights)
-        value = acc[0, t] * (keep / below)
-        for k in range(t + 1):
-            share = (weights[k] / below).astype(bf16).astype(f32)
-            value = value + share * new_keys[0, k : k + 1, :LAT].astype(f32)
-        out[0, t] = value.astype(bf16)
-
-
-def merge(queries, new_keys, acc, top, total, scale, start):
-    count, steps, heads, _ = acc.shape
+    lanes = LAT // 128
+    request = pl.program_id(0)
+
+    def one(acc, top, total):
+        for t in range(steps):
+            raw = dot(new_keys[0], queries[t, 0]) * scale
+            pad = jnp.zeros((heads - raw.shape[0], heads), f32)
+            own = jnp.concatenate([raw, pad], axis=0).T
+            highest = top[0, t]
+            columns = [own[:, k : k + 1] for k in range(t + 1)]
+            peak = highest
+            for column in columns:
+                peak = jnp.maximum(peak, column)
+            keep = jnp.exp(highest - peak)
+            weights = [jnp.exp(column - peak) for column in columns]
+            below = total[0, t] * keep + sum(weights)
+            value = acc[0, t] * (keep / below)
+            for k in range(t + 1):
+                share = (weights[k] / below).astype(bf16).astype(f32)
+                value = value + share * new_keys[0, k : k + 1, :LAT].astype(f32)
+            for j in range(lanes):
+                rows[pl.ds(j * steps + t, heads, stride=lanes * steps), :] = value[:, j * 128 : (j + 1) * 128]
+        out[0] = rows[...].astype(bf16)
+
+    @pl.when(request < count)
+    def _():
+        one(acc, top, total)
+
+    @pl.when(request >= count)
+    def _():
+        one(last_acc, last_top, last_total)
+
+
+def merge(queries, new_keys, first, last, scale):
+    count, steps, heads, _ = first[0].shape
+    rows = count + last[0].shape[0]
     width = queries.shape[2]
     per = new_keys.shape[1]
+    tall = heads * steps * LAT // 128
+
+    def early(r):
+        return (jnp.minimum(r, count - 1), 0, 0, 0)
+
+    def late(r):
+        return (jnp.maximum(r - count, 0), 0, 0, 0)
+
+    parts = [
+        pl.BlockSpec((1, steps, heads, size), where) for where in (early, late) for size in (LAT, 1, 1)
+    ]
     return pl.pallas_call(
-        functools.partial(merge_kernel, scale),
-        grid=(count,),
+        functools.partial(merge_kernel, scale, count),
+        grid=(rows,),
         in_specs=[
-            pl.BlockSpec((steps, 1, width, heads), lambda r: (0, r + start, 0, 0)),
-            pl.BlockSpec((1, per, width), lambda r: (r + start, 0, 0)),
-            pl.BlockSpec((1, steps, heads, LAT), lambda r: (r, 0, 0, 0)),
-            pl.BlockSpec((1, steps, heads, 1), lambda r: (r, 0, 0, 0)),
-            pl.BlockSpec((1, steps, heads, 1), lambda r: (r, 0, 0, 0)),
+            pl.BlockSpec((steps, 1, width, heads), lambda r: (0, r, 0, 0)),
+            pl.BlockSpec((1, per, width), lambda r: (r, 0, 0)),
+            *parts,
         ],
-        out_specs=pl.BlockSpec((1, steps, heads, LAT), lambda r: (r, 0, 0, 0)),
-        out_shape=jax.ShapeDtypeStruct((count, steps, heads, LAT), bf16),
+        out_specs=pl.BlockSpec((1, tall, 128), lambda r: (r, 0, 0)),
+        out_shape=jax.ShapeDtypeStruct((rows, tall, 128), bf16),
+        scratch_shapes=[pltpu.VMEM((tall, 128), f32)],
         compiler_params=pltpu.CompilerParams(vmem_limit_bytes=32 * 2**20),
-    )(queries, new_keys, acc, top, total)
-
-
-def project_kernel(core, hidden, own0, a0, b0, c0, own1, a1, b1, c1, gain, kv_own, kv_other, kv_gain, turns, layer, keys):
+    )(queries, new_keys, *first, *last)
+
+
+def project_kernel(core, hidden, own0, a0, b0, c0, own1, a1, b1, c1, gain, kv_own, kv_other, kv_gain, turns, layer, keys, stage):
     rows = []
     for t, (own, a, b, c) in enumerate(((own0, a0, b0, c0), (own1, a1, b1, c1))):
         mixture = own[...] + a[...].astype(f32) + b[...].astype(f32) + c[...].astype(f32)
         rows.append(hidden[t].astype(f32) + mixture)
     both = jnp.concatenate(rows, axis=0).astype(bf16)
-    layer[...] = both
+    many, width = both.shape
+    wide = both.astype(f32)
+    for k in range(width // 128):
+        for t in range(2):
+            stage[pl.ds(2 * k + t, BLOCK, stride=width // 64), :] = wide[
+                t * BLOCK : (t + 1) * BLOCK, k * 128 : (k + 1) * 128
+            ]
+    layer[...] = stage[...].astype(bf16)
     normed = rms_scale(both, gain[...]).astype(bf16)
     half = normed.shape[1] // 2
     swapped = core[0] > 0
     low, high = normed[:, :half].astype(f32), normed[:, half:].astype(f32)
     first = jnp.where(swapped, high, low).astype(bf16)
     second = jnp.where(swapped, low, high).astype(bf16)
-    projected = dot(first, kv_own[...], NT) + dot(second, kv_other[...], NT)
+    projected = (dot(kv_own[...], first, NT) + dot(kv_other[...], second, NT)).T
     keys[:, :LAT] = rms_scale(projected[:, :LAT], kv_gain[...]).astype(bf16)
     rope = projected[:, LAT:]
     crossed = jnp.concatenate([-rope[:, ROPE // 2 :], rope[:, : ROPE // 2]], axis=1)
     keys[:, LAT:] = (rope * turns[0] + crossed * turns[1]).astype(bf16)
 
 
-def spread_x(own):
+def hold(*values):
+    return lax.optimization_barrier(values)
+
+
+def steps_y(mine):
+    return [mine, shift(mine, "y", 1), shift(mine, "y", 3), shift(mine, "y", 2)]
+
+
+def steps_z(parts, sign):
+    return [parts[0]] + [shift(parts[i], "z", sign * i % SIDE) for i in (1, 2, 3)]
+
+
+def near_rows(own, left, right):
     half = own.shape[0] // 2
-    left = shift(own, "x", 1)
-    right = shift(own, "x", 3)
-    far_a = shift(left[:half], "x", 1)
-    far_b = shift(right[half:], "x", 3)
-    return [own, left, right, far_a, far_b]
-
-
-def back_x(place, summed):
-    half = SLOTS // 2
-    own, left, right, far = [summed[i * SLOTS : (i + 1) * SLOTS] for i in range(SIDE)]
-    got_a = shift(far[:half], "x", 1)
-    got_b = shift(far[half:], "x", 3)
-    from_left_b = shift(right[half:], "x", 1)
-    from_right_a = shift(left[:half], "x", 3)
-    from_left_a = shift(add(right[:half], got_a), "x", 1)
-    from_right_b = shift(add(left[half:], got_b), "x", 3)
-    outs = [((2 * PART, own.shape[1] // 2), bf16)] * SIDE
-    return call(finish_kernel, outs, place, own, from_left_a, from_right_a, from_left_b, from_right_b)
-
-
-def fresh_keys(fresh_cache, fresh_order):
-    chips = ("y", "z", "x")
-    count = lax.axis_size(chips)
-    _, width, context = fresh_cache.shape
+    return jnp.concatenate([own, left[half:], right[:half], right[half:], left[:half]], axis=0)
+
+
+CHIPS = ("y", "z", "x")
+
+
+def fresh_cut(fresh_t):
+    width, context = fresh_t.shape
+    count = lax.axis_size(CHIPS)
     tiles = width * context // 1024
     each = -(-tiles // count)
-
-    def to_tiles(array):
-        return array.reshape(width // 8, 8, context // 128, 128).swapaxes(1, 2).reshape(tiles, 8, 128)
-
-    def from_tiles(array):
-        return array.reshape(width // 8, context // 128, 8, 128).swapaxes(1, 2).reshape(width, context)
-
-    cut = jnp.pad(to_tiles(fresh_cache[0]), ((0, each * count - tiles), (0, 0), (0, 0)))
-    cut = cut.reshape(count, each * 8, 128)
-    here = lax.all_to_all(cut, chips, split_axis=0, concat_axis=0, tiled=True)
-    there = swap(here)
+    cut = fresh_t.reshape(width // 8, 8, context // 128, 128).swapaxes(1, 2).reshape(tiles, 8, 128)
+    cut = jnp.pad(cut, ((0, each * count - tiles), (0, 0), (0, 0)))
+    return cut.reshape(count, each * 8, 128)
+
+
+def fresh_join(whole, width, context):
+    tiles = width * context // 1024
+    whole = whole.reshape(-1, 8, 128)[:tiles].reshape(width // 8, context // 128, 8, 128)
+    return whole.swapaxes(1, 2).reshape(width, context)
+
+
+def fresh_sort(here, there, fresh_order):
     core = lax.axis_index("c")
+    count = here.shape[0]
     wanted = lax.dynamic_slice_in_dim(fresh_order, core * count, count, 0)
     own_core = (wanted >= count) == (core > 0)
     index = wanted % count
-    ordered = jnp.where(own_core[:, None, None], jnp.take(here, index, axis=0), jnp.take(there, index, axis=0))
-    whole = lax.all_to_all(ordered, chips, split_axis=0, concat_axis=0, tiled=True)
-    return from_tiles(whole.reshape(count * each, 8, 128)[:tiles])[None]
+    return jnp.where(
+        own_core[:, None, None], jnp.take(here, index, axis=0), jnp.take(there, index, axis=0)
+    )
+
+
+def to_chips(pieces):
+    return lax.all_to_all(pieces, CHIPS, split_axis=0, concat_axis=0, tiled=True)
 
 
 def shards(
@@ -430,42 +496,98 @@
     query_t = queries.swapaxes(2, 3)
     resident_t = resident_cache.swapaxes(1, 2)
 
-    weights = []
-    shared = []
-    for step in range(steps_count):
-        mine = payload[step]
-        held = [mine, shift(mine, "y", 1), shift(mine, "y", 3), shift(mine, "y", 2)]
+    slot_half = SLOTS // 2
+    rows = (BLOCK, model_width)
+
+    def select(held):
         *parts, weight = call(
             select_kernel, [folded] * SIDE + [((2, SIDE * 2 * PART, SIDE * BLOCK), f32)],
             pick, fixed, lower, *held,
         )
-        weights.append(weight)
-        parts = [parts[0], shift(parts[1], "z", 1), shift(parts[2], "z", 2), shift(parts[3], "z", 3)]
-        (slots,) = call(assemble_kernel, [((SLOTS, model_width), bf16)], place, *parts)
-        shared.append(spread_x(slots))
-
-    fresh_t = fresh_keys(fresh_cache.swapaxes(1, 2), fresh_order)
+        return parts, weight
+
+    def assemble(parts):
+        return call(assemble_kernel, [((SLOTS, model_width), bf16)], place, *parts)[0]
+
+    def combine(weight, parts):
+        return call(
+            combine_kernel, [(rows, f32), (rows, bf16), (rows, bf16), (rows, bf16)],
+            fixed, weight, *parts,
+        )
+
+    def back_y(own, one, two, three):
+        return [own, shift(one, "y", 3), shift(two, "y", 1), shift(three, "y", 2)]
+
+    def finish(own, plus, minus, la, rb):
+        return call(finish_kernel, [folded] * SIDE, place, own, plus, minus, la, rb)
+
+    def run_experts(near, near_swapped, far, far_swapped):
+        return experts([near, far], [near_swapped, far_swapped], expert_gate, expert_up, expert_down)
+
+    def meet(ra, lb, plus, minus):
+        return add(ra, plus[slot_half:]), add(lb, minus[slot_half:])
+
+    held = steps_y(payload[0])
+    pieces = fresh_cut(fresh_cache[0].T)
+    held, payload1, pieces = hold(held, payload[1], pieces)
+    parts, weight0 = select(held)
+    parts = steps_z(parts, 1)
+    held = steps_y(payload1)
+    here = to_chips(pieces)
+    parts, held, weight0, here = hold(parts, held, weight0, here)
+    own0 = assemble(parts)
+    left0, right0 = shift(own0, "x", 1), shift(own0, "x", 3)
+    parts, weight1 = select(held)
+    parts = steps_z(parts, 1)
+    there = swap(here)
+    past_resident = past(cache_len, query_t, resident_t, score_scale, 0)
+    own0, left0, right0, parts, weight1, here, there, past_resident = hold(
+        own0, left0, right0, parts, weight1, here, there, past_resident
+    )
+    far_a, far_b = shift(left0[:slot_half], "x", 1), shift(right0[slot_half:], "x", 3)
+    near0 = near_rows(own0, left0, right0)
+    near0_swapped = swap(near0)
+    own1 = assemble(parts)
+    sorted_pieces = fresh_sort(here, there, fresh_order)
+    far_a, far_b, near0, near0_swapped, own1, sorted_pieces = hold(
+        far_a, far_b, near0, near0_swapped, own1, sorted_pieces
+    )
+    left1, right1 = shift(own1, "x", 1), shift(own1, "x", 3)
+    far0 = jnp.concatenate([far_a, far_b], axis=0)
+    kept0, sent0 = run_experts(near0, near0_swapped, far0, swap(far0))
+    left1, right1, kept0, sent0, sorted_pieces = hold(left1, right1, kept0, sent0, sorted_pieces)
+    far_a, far_b = shift(left1[:slot_half], "x", 1), shift(right1[slot_half:], "x", 3)
+    got0 = swap(sent0)
+    near1 = near_rows(own1, left1, right1)
+    near1_swapped = swap(near1)
+    own0, lb0, ra0, plus0, minus0 = pair_sums(kept0, got0)
+    far_a, far_b, near1, near1_swapped, own0, lb0, ra0, plus0, minus0, sorted_pieces = hold(
+        far_a, far_b, near1, near1_swapped, own0, lb0, ra0, plus0, minus0, sorted_pieces
+    )
+    plus0, minus0 = shift(plus0, "x", 1), shift(minus0, "x", 3)
+    far1 = jnp.concatenate([far_a, far_b], axis=0)
+    kept1, sent1 = run_experts(near1, near1_swapped, far1, swap(far1))
+    plus0, minus0, kept1, sent1, sorted_pieces = hold(plus0, minus0, kept1, sent1, sorted_pieces)
+    ra0, lb0 = meet(ra0, lb0, plus0, minus0)
+    la0, rb0 = shift(ra0, "x", 1), shift(lb0, "x", 3)
+    got1 = swap(sent1)
+    own1, lb1, ra1, plus1, minus1 = pair_sums(kept1, got1)
+    la0, rb0, own1, lb1, ra1, plus1, minus1, sorted_pieces = hold(
+        la0, rb0, own1, lb1, ra1, plus1, minus1, sorted_pieces
+    )
+    plus1, minus1 = shift(plus1, "x", 1), shift(minus1, "x", 3)
+    parts = steps_z(finish(own0, plus0, minus0, la0, rb0), -1)
+    whole = to_chips(sorted_pieces)
+    plus1, minus1, parts, whole = hold(plus1, minus1, parts, whole)
+    ra1, lb1 = meet(ra1, lb1, plus1, minus1)
+    la1, rb1 = shift(ra1, "x", 1), shift(lb1, "x", 3)
+    mixed0 = back_y(*combine(weight0, parts))
+    fresh_t = fresh_join(whole, LAT + ROPE, fresh_cache.shape[1])[None]
+    past_fresh = past(cache_len[resident_rows:], query_t, fresh_t, score_scale, resident_rows)
+    la1, rb1, mixed0, past_fresh = hold(la1, rb1, mixed0, past_fresh)
+    parts = steps_z(finish(own1, plus1, minus1, la1, rb1), -1)
     other_down = swap(kv_down.T)
-
-    returned = []
-    for step in range(steps_count):
-        others = [swap(piece) for piece in shared[step]]
-        kept, sent = experts(shared[step], others, expert_gate, expert_up, expert_down)
-        returned.append(back_x(place, add(kept, swap(sent))))
-
-    past_resident = past(cache_len, query_t, resident_t, score_scale, 0)
-    past_fresh = past(cache_len[resident_rows:], query_t, fresh_t, score_scale, resident_rows)
-
-    mixed = []
-    for step in range(steps_count):
-        parts = returned[step]
-        parts = [parts[0], shift(parts[1], "z", 3), shift(parts[2], "z", 2), shift(parts[3], "z", 1)]
-        rows = (BLOCK, model_width)
-        own, one, two, three = call(
-            combine_kernel, [(rows, f32), (rows, bf16), (rows, bf16), (rows, bf16)],
-            fixed, weights[step], *parts,
-        )
-        mixed += [own, shift(one, "y", 3), shift(two, "y", 1), shift(three, "y", 2)]
+    mixed = mixed0 + back_y(*combine(weight1, parts))
 
     positions = jnp.pad(cache_len, (0, BLOCK - local_rows)).astype(f32)[None, :]
     positions = (positions + jnp.arange(steps_count).astype(f32)[:, None]).reshape(-1)
@@ -476,17 +598,18 @@
     many = steps_count * BLOCK
     layer, keys = call(
         project_kernel,
-        [((many, model_width), bf16), ((many, LAT + ROPE), bf16)],
+        [((many * model_width // 128, 128), bf16), ((many, LAT + ROPE), bf16)],
         core, hidden_rows, *mixed, attn_gain[None], kv_down.T, other_down, kv_gain[None], turns,
-        smem=1, limit=40,
-    )
-    layer_out = layer.reshape(steps_count, BLOCK, model_width)[:, :local_rows]
+        smem=1, limit=40, scratch=[pltpu.VMEM((many * model_width // 128, 128), f32)],
+    )
+    tall = model_width // 128
+    layer = layer[: local_rows * steps_count * tall].reshape(local_rows, tall, steps_count, 128)
+    layer_out = layer.transpose(2, 0, 1, 3).reshape(steps_count, local_rows, model_width)
     new_keys = jnp.pad(
         keys.reshape(steps_count, BLOCK, LAT + ROPE).swapaxes(0, 1), ((0, 0), (0, BLOCK - steps_count), (0, 0))
     )
-    first = merge(query_t, new_keys, *past_resident, score_scale, 0)
-    second = merge(query_t, new_keys, *past_fresh, score_scale, resident_rows)
-    attended = jnp.concatenate([first, second], axis=0).swapaxes(0, 1)
+    attended = merge(query_t, new_keys, past_resident, past_fresh, score_scale)
+    attended = attended.reshape(local_rows, -1, steps_count, 128).transpose(2, 0, 1, 3)
     return layer_out, attended.reshape(steps_count, local_rows, -1)
 
 

time: 308 us -> 259 us (0.84)
  waiting for transfers between devices: 88.3 us -> 54.3 us
  starting transfers between devices: 94.7 us -> 82.2 us
  Pallas kernels: 61.5 us -> 52.5 us
  local copies, waits for them, and re-layouts: 48.8 us -> 57.7 us
    ppermute x58 -> x48, waiting for transfers between devices: 88.3 us -> 54.3 us  [shift(): lax.ppermute(values, axis, [(i, (i + by) % size) for i in range(size)])]
    ppermute x58 -> x48, starting transfers between devices: 78.8 us -> 64.1 us  [shift(): lax.ppermute(values, axis, [(i, (i + by) % size) for i in range(size)])]
    unnamed x101 -> x134, local copies, waits for them, and re-layouts: 31.2 us -> 43.2 us
    pallas_call x2, Pallas kernels: 30.6 us -> 19 us  [experts(): pl.pallas_call(functools.partial(expert_kernel, pieces, chunks), grid=(2...]
    pallas_call x2 -> x3, Pallas kernels: 4.69 us -> 10.5 us  [the longest x1 5.77 us: merge(): pl.pallas_call(functools.partial(merge_kernel, scale, count), grid=(rows,...]
    reshape x1 -> x0, local copies, waits for them, and re-layouts: 3.58 us -> none  [shards(): return (layer_out, attended.reshape(steps_count, local_rows, -1))]
    convert_element_type x4, other arithmetic: 4.83 us -> 1.41 us  [add(): return sum((term.astype(f32) for term in terms)).astype(bf16)]
    pallas_call x9, Pallas kernels: 17.7 us -> 14.4 us  [call(): pl.pallas_call(kernel, out_shape=[jax.ShapeDtypeStruct(shape, dtype) for...]
  transfers between devices with their start and end apart: 60 -> 50, of which waited for: 22 -> 20; matrix products, arithmetic and copies ran while one was open for 7% -> 7% of each run, Pallas kernels for 12% -> 16%
where the time goes in v1:
time: 259 us; the launch traced here: 258 us
  starting transfers between devices  82.2 us (32%)
  local copies, waits for them, and re-layouts  57.7 us (22%)
  waiting for transfers between devices  54.3 us (21%)
  Pallas kernels  52.5 us (20%)
  other arithmetic  9.84 us (4%)
    ppermute x48, starting transfers between devices, shift(): lax.ppermute(values, axis, [(i, (i + by) % size) for i in range(size)])  64.1 us
    ppermute x48, waiting for transfers between devices, shift(): lax.ppermute(values, axis, [(i, (i + by) % size) for i in range(size)])  54.3 us
    unnamed x134, local copies, waits for them, and re-layouts  43.2 us
    pallas_call x2, Pallas kernels, experts(): pl.pallas_call(functools.partial(expert_kernel, pieces, chunks), grid=(2...  19 us
    all_to_all x2, starting transfers between devices, to_chips(): lax.all_to_all(pieces, CHIPS, split_axis=0, concat_axis=0, tiled=True)  18.1 us
    pallas_call x9, Pallas kernels, call(): pl.pallas_call(kernel, out_shape=[jax.ShapeDtypeStruct(shape, dtype) for...  14.4 us
    pallas_call x2, Pallas kernels, past(): pl.pallas_call(functools.partial(past_kernel, scale), grid_spec=pltpu.Pre...  8.52 us
    pallas_call x1, Pallas kernels, merge(): pl.pallas_call(functools.partial(merge_kernel, scale, count), grid=(rows,...  5.77 us
  transfers between devices with their start and end apart: 50, of which 20 were waited for; matrix products, arithmetic and copies ran while one was open for 7% of the time, Pallas kernels for 16%

profile of v1, /device:TPU:0, one launch (start us, length us, event | category | flops | bytes accessed | tf_op | source)
XLA Modules:
  0.0 257.8 jit_solution(14826415710732867298)
XLA Ops:
  12.3 2.6 collective-permute-done.2.b3
  14.9 10.3 %all-to-all-start = ((bf16[64,40,128]{2,1,0:T(8,128)(2,1)}), bf16[64,40,128]{2,1,0:T(8,128)(2,1)}, u32[]{:S(2)}, u32[]{:S(2)}) async-start(bf16[64,40,128]{2,1,0:T(8,128)(2,1)} %bitcast.51), calls=%async_computation | async-start | bytes 1310720 | tf_op jit(solution)/shard_map/all_to_all | solution.py:448
  29.8 2.7 %collective-permute-start.4 = (bf16[24,3584]{1,0:T(8,128)(2,1)S(1)}, bf16[24,3584]{1,0:T(8,128)(2,1)S(1)}, u32[]{:S(2)}, u32[]{:S(2)}) collective-permute-start(bf16[24,3584]{1,0:T(8,128)(2,1)S(1)} %get-tuple-element.136), channel_id=1, source_target_pairs={{0,8},{4,12},{8,0},{12,4},{1,9},{5,13},{9,1},{13,5},{2,10},{6,14},... | collective-permute-start | bytes 516104 | tf_op jit(solution)/shard_map/ppermute | solution.py:44
  39.4 3.5 %collective-permute-done.8.b3 = bf16[8,7296]{1,0:T(8,128)(2,1)S(1)} collective-permute-done((bf16[8,7296]{1,0:T(8,128)(2,1)S(1)}, bf16[8,7296]{1,0:T(8,128)(2,1)S(1)}, u32[]{:S(2)}, u32[]{:S(2)}) %collective-permute-start.8) | collective-permute-done | bytes 116768 | tf_op jit(solution)/shard_map/ppermute | solution.py:44
  49.3 2.7 %collective-permute-start.12 = (bf16[24,3584]{1,0:T(8,128)(2,1)S(1)}, bf16[24,3584]{1,0:T(8,128)(2,1)S(1)}, u32[]{:S(2)}, u32[]{:S(2)}) collective-permute-start(bf16[24,3584]{1,0:T(8,128)(2,1)S(1)} %get-tuple-element.151), channel_id=1, source_target_pairs={{0,8},{4,12},{8,0},{12,4},{1,9},{5,13},{9,1},{13,5},{2,10},{6,14},... | collective-permute-start | bytes 516104 | tf_op jit(solution)/shard_map/ppermute | solution.py:44
  52.0 4.1 %collective-permute-done.11.f1 = bf16[24,3584]{1,0:T(8,128)(2,1)S(1)} collective-permute-done((bf16[24,3584]{1,0:T(8,128)(2,1)S(1)}, bf16[24,3584]{1,0:T(8,128)(2,1)S(1)}, u32[]{:S(2)}, u32[]{:S(2)}) %collective-permute-start.11) | collective-permute-done | bytes 172064 | tf_op jit(solution)/shard_map/ppermute | solution.py:44
  59.7 6.8 %shard_map.197 = (f32[6,2,128,512]{3,2,1,0:T(8,128)S(1)}, f32[6,2,128,1]{3,2,1,0:T(8,128)S(1)}, f32[6,2,128,1]{3,2,1,0:T(8,128)S(1)}) custom-call(s32[7]{0:T(128)S(1)} %copy-done.60, bf16[2,7,576,128]{3,2,1,0:T(8,128)(2,1)S(1)} %bitcast.41, bf16[6,576,512]{2,1,0:T(8,128)(2,1)S(1)} %bitcast.50), custom_call_target="tpu_custom_call" | custom-call | flops 1711276032 | bytes 8454144 | tf_op jit(solution)/shard_map/pallas_call | solution.py:278
  72.5 2.4 collective-permute-start.16
  75.0 2.6 %gather_fusion = bf16[64,40,128]{2,1,0:T(8,128)(2,1)} fusion(bf16[64,40,128]{2,1,0:T(8,128)(2,1)} %all-to-all-done, s32[1024]{0:T(1024)S(1)} %pad_clamp_fusion), kind=kCustom, calls=%fused_computation.clone | custom fusion | bytes 1310976 | tf_op jit(solution)/shard_map/jit(_take)/gather | solution.py:443
  77.5 2.6 gather_fusion.1
  81.0 2.6 %select_select_fusion = bf16[64,40,128]{2,1,0:T(8,128)(2,1)} fusion(bf16[64,40,128]{2,1,0:T(8,128)(2,1)} %gather_fusion.1, bf16[64,40,128]{2,1,0:T(8,128)(2,1)} %gather_fusion, pred[64]{0:T(512)(128)(4,1)S(1)} %get-tuple-element.257, pred[64]{0:T(512)(128)(4,1)S(1)} %get-tuple-element.271), kind=kLoop, calls=%fused_computation.8 | loop fusion | flops 983040 | bytes 1966208 | tf_op jit(solution)/shard_map/jit(_where)/select_n | solution.py:442
  93.5 10.5 %shard_map.199 = (bf16[192,7168]{1,0:T(8,128)(2,1)S(1)}, bf16[192,7168]{1,0:T(8,128)(2,1)S(1)}) custom-call(bf16[144,7168]{1,0:T(8,128)(2,1)} %pad_maximum_fusion.refs_0_, bf16[48,7168]{1,0:T(8,128)(2,1)S(1)} %constant_dynamic-update-slice_fusion.refs_1_, bf16[144,7168]{1,0:T(8,128)(2,1)} %collective-permute-done.17.refs_2_, ...), custom_call_target="tpu_custom_call" | custom-call | flops 4227858432 | bytes 22020096 | tf_op jit(solution)/shard_map/pallas_call | solution.py:239
  112.4 4.8 %collective-permute-done.21 = bf16[24,7168]{1,0:T(8,128)(2,1)S(1)} collective-permute-done((bf16[24,7168]{1,0:T(8,128)(2,1)S(1)}, bf16[24,7168]{1,0:T(8,128)(2,1)S(1)}, u32[]{:S(2)}, u32[]{:S(2)}) %collective-permute-start.21) | collective-permute-done | bytes 344096 | tf_op jit(solution)/shard_map/ppermute | solution.py:44
  123.5 8.6 %shard_map.201 = (bf16[192,7168]{1,0:T(8,128)(2,1)S(1)}, bf16[192,7168]{1,0:T(8,128)(2,1)S(1)}) custom-call(bf16[144,7168]{1,0:T(8,128)(2,1)S(1)} %pad_maximum_fusion.1.refs_0_, bf16[48,7168]{1,0:T(8,128)(2,1)S(1)} %constant_dynamic-update-slice_fusion.2.refs_1_, bf16[144,7168]{1,0:T(8,128)(2,1)S(1)} %copy-done.11, ...), custom_call_target="tpu_custom_call" | custom-call | flops 4227858432 | bytes 22020096 | tf_op jit(solution)/shard_map/pallas_call | solution.py:239
  132.1 5.7 %collective-permute-done.25.plus = bf16[48,7168]{1,0:T(8,128)(2,1)S(1)} collective-permute-done((bf16[48,7168]{1,0:T(8,128)(2,1)S(1)}, bf16[48,7168]{1,0:T(8,128)(2,1)S(1)}, u32[]{:S(2)}, u32[]{:S(2)}) %collective-permute-start.25) | collective-permute-done | bytes 688160 | tf_op jit(solution)/shard_map/ppermute | solution.py:44
  138.0 2.9 %collective-permute-start.29 = (bf16[24,7168]{1,0:T(8,128)(2,1)S(1)}, bf16[24,7168]{1,0:T(8,128)(2,1)S(1)}, u32[]{:S(2)}, u32[]{:S(2)}) collective-permute-start(bf16[24,7168]{1,0:T(8,128)(2,1)S(1)} %add_convert_fusion.2), channel_id=1, source_target_pairs={{0,3},{1,0},{2,1},{3,2},{4,7},{5,4},{6,5},{7,6},{8,11},{9,8},{10,9... | collective-permute-start | bytes 1032200 | tf_op jit(solution)/shard_map/ppermute | solution.py:44
  143.0 3.4 %shard_map.202 = (bf16[48,7168]{1,0:T(8,128)(2,1)S(1)}, bf16[24,7168]{1,0:T(8,128)(2,1)S(1)}, bf16[24,7168]{1,0:T(8,128)(2,1)S(1)}, bf16[48,7168]{1,0:T(8,128)(2,1)}, bf16[48,7168]{1,0:T(8,128)(2,1)}) custom-call(bf16[192,7168]{1,0:T(8,128)(2,1)S(1)} %get-tuple-element.198.kept, bf16[192,7168]{1,0:T(8,128)(2,1)S(1)} %collective-permute-done.30.got), custom_call_target="tpu_custom_call" | custom-call | flops 1376256 | bytes 8257536 | tf_op jit(solution)/shard_map/pallas_call | solution.py:161
  149.7 2.8 %collective-permute-done.28.la = bf16[24,7168]{1,0:T(8,128)(2,1)S(1)} collective-permute-done((bf16[24,7168]{1,0:T(8,128)(2,1)S(1)}, bf16[24,7168]{1,0:T(8,128)(2,1)S(1)}, u32[]{:S(2)}, u32[]{:S(2)}) %collective-permute-start.28) | collective-permute-done | bytes 344096 | tf_op jit(solution)/shard_map/ppermute | solution.py:44
  153.3 3.2 %collective-permute-start.32 = (bf16[48,7168]{1,0:T(8,128)(2,1)}, bf16[48,7168]{1,0:T(8,128)(2,1)}, u32[]{:S(2)}, u32[]{:S(2)}) collective-permute-start(bf16[48,7168]{1,0:T(8,128)(2,1)} %get-tuple-element.208), channel_id=1, source_target_pairs={{0,3},{1,0},{2,1},{3,2},{4,7},{5,4},{6,5},{7,6},{8,11},{9,8},{10,9... | collective-permute-start | bytes 2064392 | tf_op jit(solution)/shard_map/ppermute | solution.py:44
  156.5 7.8 %all-to-all-start.1 = ((bf16[64,40,128]{2,1,0:T(8,128)(2,1)}), bf16[64,40,128]{2,1,0:T(8,128)(2,1)}, u32[]{:S(2)}, u32[]{:S(2)}) async-start(bf16[64,40,128]{2,1,0:T(8,128)(2,1)} %select_select_fusion), calls=%async_computation.1 | async-start | bytes 1310720 | tf_op jit(solution)/shard_map/all_to_all | solution.py:448
  170.3 2.8 %collective-permute-start.33 = (bf16[24,3584]{1,0:T(8,128)(2,1)S(1)}, bf16[24,3584]{1,0:T(8,128)(2,1)S(1)}, u32[]{:S(2)}, u32[]{:S(2)}) collective-permute-start(bf16[24,3584]{1,0:T(8,128)(2,1)S(1)} %get-tuple-element.213), channel_id=1, source_target_pairs={{0,12},{4,0},{8,4},{12,8},{1,13},{5,1},{9,5},{13,9},{2,14},{6,2},{... | collective-permute-start | bytes 516104 | tf_op jit(solution)/shard_map/ppermute | solution.py:44
  174.8 8.6 %collective-permute-done.33.f1 = bf16[24,3584]{1,0:T(8,128)(2,1)S(1)} collective-permute-done((bf16[24,3584]{1,0:T(8,128)(2,1)S(1)}, bf16[24,3584]{1,0:T(8,128)(2,1)S(1)}, u32[]{:S(2)}, u32[]{:S(2)}) %collective-permute-start.33) | collective-permute-done | bytes 172064 | tf_op jit(solution)/shard_map/ppermute | solution.py:44
  195.1 2.3 collective-permute-start.38
  198.0 2.2 collective-permute-done.38.a0
  200.8 2.9 %collective-permute-start.40 = (bf16[8,7168]{1,0:T(8,128)(2,1)S(1)}, bf16[8,7168]{1,0:T(8,128)(2,1)S(1)}, u32[]{:S(2)}, u32[]{:S(2)}) collective-permute-start(bf16[8,7168]{1,0:T(8,128)(2,1)S(1)} %get-tuple-element.228), channel_id=1, source_target_pairs={{0,32},{16,48},{32,0},{48,16},{1,33},{17,49},{33,1},{49,17},{2,34}... | collective-permute-start | bytes 344072 | tf_op jit(solution)/shard_map/ppermute | solution.py:44
  208.5 2.5 shard_map.206
  211.7 3.7 %collective-permute-start.41 = (bf16[24,3584]{1,0:T(8,128)(2,1)}, bf16[24,3584]{1,0:T(8,128)(2,1)S(1)}, u32[]{:S(2)}, u32[]{:S(2)}) collective-permute-start(bf16[24,3584]{1,0:T(8,128)(2,1)} %get-tuple-element.242), channel_id=1, source_target_pairs={{0,12},{4,0},{8,4},{12,8},{1,13},{5,1},{9,5},{13,9},{2,14},{6,2},{... | collective-permute-start | bytes 516104 | tf_op jit(solution)/shard_map/ppermute | solution.py:44
  216.9 5.4 %collective-permute-done.41.f1 = bf16[24,3584]{1,0:T(8,128)(2,1)S(1)} collective-permute-done((bf16[24,3584]{1,0:T(8,128)(2,1)}, bf16[24,3584]{1,0:T(8,128)(2,1)S(1)}, u32[]{:S(2)}, u32[]{:S(2)}) %collective-permute-start.41) | collective-permute-done | bytes 172064 | tf_op jit(solution)/shard_map/ppermute | solution.py:44
  238.1 2.2 collective-permute-done.45.b1
  240.4 2.2 copy-done.6
  246.2 5.0 %shard_map.208 = (bf16[896,128]{1,0:T(8,128)(2,1)S(1)}, bf16[16,576]{1,0:T(8,128)(2,1)S(1)}) custom-call(s32[1]{0:T(128)} %bitcast.core, bf16[2,8,7168]{2,1,0:T(8,128)(2,1)S(1)} %pad.20.hidden, f32[8,7168]{1,0:T(8,128)S(1)} %copy-done.31, bf16[8,7168]{1,0:T(8,128)(2,1)S(1)} %copy-done.47, bf16[8,7168]{1,0:T(8,128)(2,1)S(1)} %copy-done.49, ...), custom_call_target="tpu_custom_call" | custom-call | bytes 9672708 | tf_op jit(solution)/shard_map/pallas_call | solution.py:63
  252.0 5.8 %shard_map.209 = bf16[7,1024,128]{2,1,0:T(8,128)(2,1)} custom-call(bf16[2,7,576,128]{3,2,1,0:T(8,128)(2,1)S(1)} %bitcast.43, bf16[8,8,576]{2,1,0:T(8,128)(2,1)S(1)} %pad.24.new_keys, f32[6,2,128,512]{3,2,1,0:T(8,128)S(1)} %copy-done.8, f32[6,2,128,1]{3,2,1,0:T(8,128)S(1)} %copy-done.18, f32[6,2,128,1]{3,2,1,0:T(8,128)S(1)} %copy-done.20, ...), custom_call_target="tpu_custom_call" | custom-call | tf_op jit(solution)/shard_map/pallas_call | solution.py:358
  (266 shorter events, 118.3 us)
Async XLA Ops:
  14.9 28.8 %all-to-all-start = ((bf16[64,40,128]{2,1,0:T(8,128)(2,1)}), bf16[64,40,128]{2,1,0:T(8,128)(2,1)}, u32[]{:S(2)}, u32[]{:S(2)}) async-start(bf16[64,40,128]{2,1,0:T(8,128)(2,1)} %bitcast.51), calls=%async_computation | async-start | bytes 1310720 | tf_op jit(solution)/shard_map/all_to_all | solution.py:448
  25.3 11.3 %collective-permute-start.6 = (bf16[8,7296]{1,0:T(8,128)(2,1)S(1)}, bf16[8,7296]{1,0:T(8,128)(2,1)S(1)}, u32[]{:S(2)}, u32[]{:S(2)}) collective-permute-start(bf16[8,7296]{1,0:T(8,128)(2,1)S(1)} %get-tuple-element.145.b0), channel_id=1, source_target_pairs={{0,16},{16,32},{32,48},{48,0},{1,17},{17,33},{33,49},{49,1},{2,18}... | collective-permute-start | bytes 350216 | tf_op jit(solution)/shard_map/ppermute | solution.py:44
  28.3 14.6 %collective-permute-start.3 = (bf16[24,3584]{1,0:T(8,128)(2,1)S(1)}, bf16[24,3584]{1,0:T(8,128)(2,1)S(1)}, u32[]{:S(2)}, u32[]{:S(2)}) collective-permute-start(bf16[24,3584]{1,0:T(8,128)(2,1)S(1)} %get-tuple-element.135), channel_id=1, source_target_pairs={{0,4},{4,8},{8,12},{12,0},{1,5},{5,9},{9,13},{13,1},{2,6},{6,10},{... | collective-permute-start | bytes 516104 | tf_op jit(solution)/shard_map/ppermute | solution.py:44
  29.8 13.9 %collective-permute-start.4 = (bf16[24,3584]{1,0:T(8,128)(2,1)S(1)}, bf16[24,3584]{1,0:T(8,128)(2,1)S(1)}, u32[]{:S(2)}, u32[]{:S(2)}) collective-permute-start(bf16[24,3584]{1,0:T(8,128)(2,1)S(1)} %get-tuple-element.136), channel_id=1, source_target_pairs={{0,8},{4,12},{8,0},{12,4},{1,9},{5,13},{9,1},{13,5},{2,10},{6,14},... | collective-permute-start | bytes 516104 | tf_op jit(solution)/shard_map/ppermute | solution.py:44
  32.6 11.1 %collective-permute-start.5 = (bf16[24,3584]{1,0:T(8,128)(2,1)S(1)}, bf16[24,3584]{1,0:T(8,128)(2,1)S(1)}, u32[]{:S(2)}, u32[]{:S(2)}) collective-permute-start(bf16[24,3584]{1,0:T(8,128)(2,1)S(1)} %get-tuple-element.137), channel_id=1, source_target_pairs={{0,12},{4,0},{8,4},{12,8},{1,13},{5,1},{9,5},{13,9},{2,14},{6,2},{... | collective-permute-start | bytes 516104 | tf_op jit(solution)/shard_map/ppermute | solution.py:44
  44.5 22.1 %collective-permute-start.10 = (bf16[48,7168]{1,0:T(8,128)(2,1)S(1)}, bf16[48,7168]{1,0:T(8,128)(2,1)S(1)}, u32[]{:S(2)}, u32[]{:S(2)}) collective-permute-start(bf16[48,7168]{1,0:T(8,128)(2,1)S(1)} %shard_map.195), channel_id=1, source_target_pairs={{0,3},{1,0},{2,1},{3,2},{4,7},{5,4},{6,5},{7,6},{8,11},{9,8},{10,9... | collective-permute-start | bytes 2064392 | tf_op jit(solution)/shard_map/ppermute | solution.py:44
  46.7 19.9 %collective-permute-start.9 = (bf16[48,7168]{1,0:T(8,128)(2,1)S(1)}, bf16[48,7168]{1,0:T(8,128)(2,1)S(1)}, u32[]{:S(2)}, u32[]{:S(2)}) collective-permute-start(bf16[48,7168]{1,0:T(8,128)(2,1)S(1)} %shard_map.195), channel_id=1, source_target_pairs={{0,1},{1,2},{2,3},{3,0},{4,5},{5,6},{6,7},{7,4},{8,9},{9,10},{10,1... | collective-permute-start | bytes 2064392 | tf_op jit(solution)/shard_map/ppermute | solution.py:44
  46.7 19.9 %collective-permute-start.14 = (bf16[64,40,128]{2,1,0:T(8,128)(2,1)}, bf16[64,40,128]{2,1,0:T(8,128)(2,1)S(1)}, u32[]{:S(2)}, u32[]{:S(2)}) collective-permute-start(bf16[64,40,128]{2,1,0:T(8,128)(2,1)} %all-to-all-done), channel_id=1, source_target_pairs={{0,64},{64,0},{1,65},{65,1},{2,66},{66,2},{3,67},{67,3},{4,68},{68... | collective-permute-start | bytes 1966088 | tf_op jit(solution)/shard_map/ppermute | solution.py:44
  49.3 17.3 %collective-permute-start.12 = (bf16[24,3584]{1,0:T(8,128)(2,1)S(1)}, bf16[24,3584]{1,0:T(8,128)(2,1)S(1)}, u32[]{:S(2)}, u32[]{:S(2)}) collective-permute-start(bf16[24,3584]{1,0:T(8,128)(2,1)S(1)} %get-tuple-element.151), channel_id=1, source_target_pairs={{0,8},{4,12},{8,0},{12,4},{1,9},{5,13},{9,1},{13,5},{2,10},{6,14},... | collective-permute-start | bytes 516104 | tf_op jit(solution)/shard_map/ppermute | solution.py:44
  56.1 10.5 %collective-permute-start.13 = (bf16[24,3584]{1,0:T(8,128)(2,1)S(1)}, bf16[24,3584]{1,0:T(8,128)(2,1)S(1)}, u32[]{:S(2)}, u32[]{:S(2)}) collective-permute-start(bf16[24,3584]{1,0:T(8,128)(2,1)S(1)} %get-tuple-element.152), channel_id=1, source_target_pairs={{0,12},{4,0},{8,4},{12,8},{1,13},{5,1},{9,5},{13,9},{2,14},{6,2},{... | collective-permute-start | bytes 516104 | tf_op jit(solution)/shard_map/ppermute | solution.py:44
  69.8 13.8 %collective-permute-start.17 = (bf16[144,7168]{1,0:T(8,128)(2,1)}, bf16[144,7168]{1,0:T(8,128)(2,1)}, u32[]{:S(2)}, u32[]{:S(2)}) collective-permute-start(bf16[144,7168]{1,0:T(8,128)(2,1)} %pad_maximum_fusion.refs_0_), channel_id=1, source_target_pairs={{0,64},{64,0},{1,65},{65,1},{2,66},{66,2},{3,67},{67,3},{4,68},{68... | collective-permute-start | bytes 6193160 | tf_op jit(solution)/shard_map/ppermute | solution.py:44
  69.9 13.7 %collective-permute-start.15 = (bf16[24,7168]{1,0:T(8,128)(2,1)S(1)}, bf16[24,7168]{1,0:T(8,128)(2,1)}, u32[]{:S(2)}, u32[]{:S(2)}) collective-permute-start(bf16[24,7168]{1,0:T(8,128)(2,1)S(1)} %get-tuple-element.266), channel_id=1, source_target_pairs={{0,1},{1,2},{2,3},{3,0},{4,5},{5,6},{6,7},{7,4},{8,9},{9,10},{10,1... | collective-permute-start | bytes 1032200 | tf_op jit(solution)/shard_map/ppermute | solution.py:44
  72.5 11.0 %collective-permute-start.16 = (bf16[24,7168]{1,0:T(8,128)(2,1)}, bf16[24,7168]{1,0:T(8,128)(2,1)}, u32[]{:S(2)}, u32[]{:S(2)}) collective-permute-start(bf16[24,7168]{1,0:T(8,128)(2,1)} %slice.56), channel_id=1, source_target_pairs={{0,3},{1,0},{2,1},{3,2},{4,7},{5,4},{6,5},{7,6},{8,11},{9,8},{10,9... | collective-permute-start | bytes 1032200 | tf_op jit(solution)/shard_map/ppermute | solution.py:44
  85.9 19.3 %collective-permute-start.18 = (bf16[48,7168]{1,0:T(8,128)(2,1)S(1)}, bf16[48,7168]{1,0:T(8,128)(2,1)S(1)}, u32[]{:S(2)}, u32[]{:S(2)}) collective-permute-start(bf16[48,7168]{1,0:T(8,128)(2,1)S(1)} %shard_map.198), channel_id=1, source_target_pairs={{0,1},{1,2},{2,3},{3,0},{4,5},{5,6},{6,7},{7,4},{8,9},{9,10},{10,1... | collective-permute-start | bytes 2064392 | tf_op jit(solution)/shard_map/ppermute | solution.py:44
  87.3 17.9 %collective-permute-start.19 = (bf16[48,7168]{1,0:T(8,128)(2,1)S(1)}, bf16[48,7168]{1,0:T(8,128)(2,1)S(1)}, u32[]{:S(2)}, u32[]{:S(2)}) collective-permute-start(bf16[48,7168]{1,0:T(8,128)(2,1)S(1)} %shard_map.198), channel_id=1, source_target_pairs={{0,3},{1,0},{2,1},{3,2},{4,7},{5,4},{6,5},{7,6},{8,11},{9,8},{10,9... | collective-permute-start | bytes 2064392 | tf_op jit(solution)/shard_map/ppermute | solution.py:44
  105.3 11.9 %collective-permute-start.23 = (bf16[144,7168]{1,0:T(8,128)(2,1)S(1)}, bf16[144,7168]{1,0:T(8,128)(2,1)S(1)}, u32[]{:S(2)}, u32[]{:S(2)}) collective-permute-start(bf16[144,7168]{1,0:T(8,128)(2,1)S(1)} %pad_maximum_fusion.1.refs_0_), channel_id=1, source_target_pairs={{0,64},{64,0},{1,65},{65,1},{2,66},{66,2},{3,67},{67,3},{4,68},{68... | collective-permute-start | bytes 6193160 | tf_op jit(solution)/shard_map/ppermute | solution.py:44
  105.9 11.3 %collective-permute-start.21 = (bf16[24,7168]{1,0:T(8,128)(2,1)S(1)}, bf16[24,7168]{1,0:T(8,128)(2,1)S(1)}, u32[]{:S(2)}, u32[]{:S(2)}) collective-permute-start(bf16[24,7168]{1,0:T(8,128)(2,1)S(1)} %get-tuple-element.264), channel_id=1, source_target_pairs={{0,1},{1,2},{2,3},{3,0},{4,5},{5,6},{6,7},{7,4},{8,9},{9,10},{10,1... | collective-permute-start | bytes 1032200 | tf_op jit(solution)/shard_map/ppermute | solution.py:44
  118.6 19.2 %collective-permute-start.25 = (bf16[48,7168]{1,0:T(8,128)(2,1)S(1)}, bf16[48,7168]{1,0:T(8,128)(2,1)S(1)}, u32[]{:S(2)}, u32[]{:S(2)}) collective-permute-start(bf16[48,7168]{1,0:T(8,128)(2,1)S(1)} %get-tuple-element.186), channel_id=1, source_target_pairs={{0,1},{1,2},{2,3},{3,0},{4,5},{5,6},{6,7},{7,4},{8,9},{9,10},{10,1... | collective-permute-start | bytes 2064392 | tf_op jit(solution)/shard_map/ppermute | solution.py:44
  120.2 17.6 %collective-permute-start.26 = (bf16[48,7168]{1,0:T(8,128)(2,1)S(1)}, bf16[48,7168]{1,0:T(8,128)(2,1)S(1)}, u32[]{:S(2)}, u32[]{:S(2)}) collective-permute-start(bf16[48,7168]{1,0:T(8,128)(2,1)S(1)} %get-tuple-element.187), channel_id=1, source_target_pairs={{0,3},{1,0},{2,1},{3,2},{4,7},{5,4},{6,5},{7,6},{8,11},{9,8},{10,9... | collective-permute-start | bytes 2064392 | tf_op jit(solution)/shard_map/ppermute | solution.py:44
  138.0 10.9 %collective-permute-start.29 = (bf16[24,7168]{1,0:T(8,128)(2,1)S(1)}, bf16[24,7168]{1,0:T(8,128)(2,1)S(1)}, u32[]{:S(2)}, u32[]{:S(2)}) collective-permute-start(bf16[24,7168]{1,0:T(8,128)(2,1)S(1)} %add_convert_fusion.2), channel_id=1, source_target_pairs={{0,3},{1,0},{2,1},{3,2},{4,7},{5,4},{6,5},{7,6},{8,11},{9,8},{10,9... | collective-permute-start | bytes 1032200 | tf_op jit(solution)/shard_map/ppermute | solution.py:44
  141.0 11.5 %collective-permute-start.28 = (bf16[24,7168]{1,0:T(8,128)(2,1)S(1)}, bf16[24,7168]{1,0:T(8,128)(2,1)S(1)}, u32[]{:S(2)}, u32[]{:S(2)}) collective-permute-start(bf16[24,7168]{1,0:T(8,128)(2,1)S(1)} %add_convert_fusion.3), channel_id=1, source_target_pairs={{0,1},{1,2},{2,3},{3,0},{4,5},{5,6},{6,7},{7,4},{8,9},{9,10},{10,1... | collective-permute-start | bytes 1032200 | tf_op jit(solution)/shard_map/ppermute | solution.py:44
  153.3 32.9 %collective-permute-start.31 = (bf16[48,7168]{1,0:T(8,128)(2,1)}, bf16[48,7168]{1,0:T(8,128)(2,1)S(1)}, u32[]{:S(2)}, u32[]{:S(2)}) collective-permute-start(bf16[48,7168]{1,0:T(8,128)(2,1)} %get-tuple-element.207), channel_id=1, source_target_pairs={{0,1},{1,2},{2,3},{3,0},{4,5},{5,6},{6,7},{7,4},{8,9},{9,10},{10,1... | collective-permute-start | bytes 2064392 | tf_op jit(solution)/shard_map/ppermute | solution.py:44
  153.3 32.9 %collective-permute-start.32 = (bf16[48,7168]{1,0:T(8,128)(2,1)}, bf16[48,7168]{1,0:T(8,128)(2,1)}, u32[]{:S(2)}, u32[]{:S(2)}) collective-permute-start(bf16[48,7168]{1,0:T(8,128)(2,1)} %get-tuple-element.208), channel_id=1, source_target_pairs={{0,3},{1,0},{2,1},{3,2},{4,7},{5,4},{6,5},{7,6},{8,11},{9,8},{10,9... | collective-permute-start | bytes 2064392 | tf_op jit(solution)/shard_map/ppermute | solution.py:44
  156.5 29.7 %all-to-all-start.1 = ((bf16[64,40,128]{2,1,0:T(8,128)(2,1)}), bf16[64,40,128]{2,1,0:T(8,128)(2,1)}, u32[]{:S(2)}, u32[]{:S(2)}) async-start(bf16[64,40,128]{2,1,0:T(8,128)(2,1)} %select_select_fusion), calls=%async_computation.1 | async-start | bytes 1310720 | tf_op jit(solution)/shard_map/all_to_all | solution.py:448
  170.3 13.1 %collective-permute-start.33 = (bf16[24,3584]{1,0:T(8,128)(2,1)S(1)}, bf16[24,3584]{1,0:T(8,128)(2,1)S(1)}, u32[]{:S(2)}, u32[]{:S(2)}) collective-permute-start(bf16[24,3584]{1,0:T(8,128)(2,1)S(1)} %get-tuple-element.213), channel_id=1, source_target_pairs={{0,12},{4,0},{8,4},{12,8},{1,13},{5,1},{9,5},{13,9},{2,14},{6,2},{... | collective-permute-start | bytes 516104 | tf_op jit(solution)/shard_map/ppermute | solution.py:44
  173.1 11.0 %collective-permute-start.34 = (bf16[24,3584]{1,0:T(8,128)(2,1)S(1)}, bf16[24,3584]{1,0:T(8,128)(2,1)S(1)}, u32[]{:S(2)}, u32[]{:S(2)}) collective-permute-start(bf16[24,3584]{1,0:T(8,128)(2,1)S(1)} %get-tuple-element.214), channel_id=1, source_target_pairs={{0,8},{4,12},{8,0},{12,4},{1,9},{5,13},{9,1},{13,5},{2,10},{6,14},... | collective-permute-start | bytes 516104 | tf_op jit(solution)/shard_map/ppermute | solution.py:44
  173.9 11.6 %collective-permute-start.35 = (bf16[24,3584]{1,0:T(8,128)(2,1)S(1)}, bf16[24,3584]{1,0:T(8,128)(2,1)S(1)}, u32[]{:S(2)}, u32[]{:S(2)}) collective-permute-start(bf16[24,3584]{1,0:T(8,128)(2,1)S(1)} %get-tuple-element.215), channel_id=1, source_target_pairs={{0,4},{4,8},{8,12},{12,0},{1,5},{5,9},{9,13},{13,1},{2,6},{6,10},{... | collective-permute-start | bytes 516104 | tf_op jit(solution)/shard_map/ppermute | solution.py:44
  184.1 54.1 %collective-permute-start.47 = (bf16[576,3584]{1,0:T(8,128)(2,1)}, bf16[576,3584]{1,0:T(8,128)(2,1)}, u32[]{:S(2)}, u32[]{:S(2)}) collective-permute-start(bf16[576,3584]{1,0:T(8,128)(2,1)} %bitcast.44), channel_id=1, source_target_pairs={{0,64},{64,0},{1,65},{65,1},{2,66},{66,2},{3,67},{67,3},{4,68},{68... | collective-permute-start | bytes 12386312 | tf_op jit(solution)/shard_map/ppermute | solution.py:44
  187.4 21.1 %collective-permute-start.37 = (bf16[24,7168]{1,0:T(8,128)(2,1)S(1)}, bf16[24,7168]{1,0:T(8,128)(2,1)S(1)}, u32[]{:S(2)}, u32[]{:S(2)}) collective-permute-start(bf16[24,7168]{1,0:T(8,128)(2,1)S(1)} %add_convert_fusion), channel_id=1, source_target_pairs={{0,3},{1,0},{2,1},{3,2},{4,7},{5,4},{6,5},{7,6},{8,11},{9,8},{10,9... | collective-permute-start | bytes 1032200 | tf_op jit(solution)/shard_map/ppermute | solution.py:44
  189.4 19.1 %collective-permute-start.36 = (bf16[24,7168]{1,0:T(8,128)(2,1)S(1)}, bf16[24,7168]{1,0:T(8,128)(2,1)S(1)}, u32[]{:S(2)}, u32[]{:S(2)}) collective-permute-start(bf16[24,7168]{1,0:T(8,128)(2,1)S(1)} %add_convert_fusion.1), channel_id=1, source_target_pairs={{0,1},{1,2},{2,3},{3,0},{4,5},{5,6},{6,7},{7,4},{8,9},{9,10},{10,1... | collective-permute-start | bytes 1032200 | tf_op jit(solution)/shard_map/ppermute | solution.py:44
  211.7 10.6 %collective-permute-start.41 = (bf16[24,3584]{1,0:T(8,128)(2,1)}, bf16[24,3584]{1,0:T(8,128)(2,1)S(1)}, u32[]{:S(2)}, u32[]{:S(2)}) collective-permute-start(bf16[24,3584]{1,0:T(8,128)(2,1)} %get-tuple-element.242), channel_id=1, source_target_pairs={{0,12},{4,0},{8,4},{12,8},{1,13},{5,1},{9,5},{13,9},{2,14},{6,2},{... | collective-permute-start | bytes 516104 | tf_op jit(solution)/shard_map/ppermute | solution.py:44
  215.4 10.2 %collective-permute-start.43 = (bf16[24,3584]{1,0:T(8,128)(2,1)}, bf16[24,3584]{1,0:T(8,128)(2,1)S(1)}, u32[]{:S(2)}, u32[]{:S(2)}) collective-permute-start(bf16[24,3584]{1,0:T(8,128)(2,1)} %get-tuple-element.244), channel_id=1, source_target_pairs={{0,4},{4,8},{8,12},{12,0},{1,5},{5,9},{9,13},{13,1},{2,6},{6,10},{... | collective-permute-start | bytes 516104 | tf_op jit(solution)/shard_map/ppermute | solution.py:44
  (83 other events, 569.2 us)

commit v2 on v1

--- a/solution.py
+++ b/solution.py
@@ -56,7 +56,7 @@
     return lax.dot_general(a, b, dims, preferred_element_type=f32)
 
 
-def call(kernel, outs, *args, smem=0, flops=0, limit=32, scratch=()):
+def call(kernel, outs, *args, smem=0, flops=0, limit=12, scratch=()):
     specs = [pl.BlockSpec(memory_space=pltpu.SMEM)] * smem
     specs += [pl.BlockSpec(memory_space=pltpu.VMEM)] * (len(args) - smem)
     moved = sum(a.size * a.dtype.itemsize for a in args)
@@ -71,63 +71,94 @@
     )(*args)
 
 
-FOLD_ROW = np.arange(SIDE * 2 * PART)
-FOLD_BLOCK = FOLD_ROW // (2 * PART)
-FOLD_HALF = FOLD_ROW % (2 * PART) // PART
-FOLD_SLOT = FOLD_ROW % PART
-PLACE = np.stack(
-    [
-        (np.arange(SLOTS)[:, None] == (FOLD_BLOCK * PART + FOLD_SLOT)[None, :]) & (FOLD_HALF == half)[None, :]
-        for half in (0, 1)
-    ]
-).astype(np.float32)
-
-
-def fold_tables():
-    expert = lax.axis_index("y") * SIDE + (lax.axis_index("z") + FOLD_BLOCK) % SIDE
-    lanes = jnp.arange(META)[None, :]
-    pick = jnp.stack([expert[:, None] == lanes, expert[:, None] + EXPERTS == lanes]).astype(bf16)
-    columns = np.arange(SIDE * BLOCK)
-    same = ((FOLD_SLOT // CAP)[:, None] == (columns // BLOCK)[None, :]).astype(np.float32)
-    turn = np.broadcast_to((FOLD_SLOT % CAP)[:, None], same.shape).astype(np.float32)
-    half = np.broadcast_to(FOLD_HALF[:, None], same.shape).astype(np.float32)
-    lower = (columns[None, :] < columns[:, None]) & (
-        columns[None, :] // BLOCK == columns[:, None] // BLOCK
-    )
-    return pick, jnp.asarray(np.stack([same, turn, half])), jnp.asarray(lower.astype(np.float32), bf16)
-
-
-def select_kernel(pick, fixed, lower, b0, b1, b2, b3, o0, o1, o2, o3, weights):
-    held = jnp.concatenate([b[...].astype(f32) for b in (b0, b1, b2, b3)], axis=0)
+def row_of(shape, dim):
+    return lax.broadcasted_iota(jnp.int32, shape, dim)
+
+
+def digits(value, base, count):
+    high = sum(jnp.where(value >= base * i, 1, 0) for i in range(1, count))
+    return high, value - base * high
+
+
+def placed(half, block):
+    slot = row_of((SLOTS, 2 * PART), 0) - block * PART
+    return jnp.where((row_of((SLOTS, 2 * PART), 1) - half * PART == slot) & (slot >= 0) & (slot < PART), 1.0, 0.0).astype(bf16)
+
+
+def prepare_kernel(ids, route, hidden, gain, out, plain):
+    count, steps, width = hidden.shape
+    both = hidden[...].astype(f32)
+    blank = jnp.zeros((META - EXPERTS, META), f32)
+    spare = jnp.zeros((BLOCK - count, width), f32)
+    normed, metas, held = [], [], []
+    for t in range(steps):
+        values = both[:, t, :]
+        held += [values, spare]
+        normed += [rms_scale(values, gain[...]), spare]
+        share = route[t] / jnp.sum(route[t], axis=0, keepdims=True) * route_scaling
+        expert = lax.broadcasted_iota(jnp.int32, (EXPERTS, count), 0)
+        dense = jnp.zeros((EXPERTS, count), f32)
+        for k in range(share.shape[0]):
+            dense = dense + jnp.where(ids[t, k : k + 1] == expert, share[k : k + 1], 0.0)
+        dense = jnp.concatenate([dense, jnp.zeros((EXPERTS, META - count), f32)], axis=1)
+        dense = jnp.concatenate([dense, blank], axis=0).T
+        high = dense.astype(bf16)
+        low = (dense - high.astype(f32))[:, :EXPERTS].astype(bf16).astype(f32)
+        meta = jnp.concatenate([high.astype(f32)[:, :EXPERTS], low, blank.T[:, EXPERTS:]], axis=1)
+        metas.append(meta[:BLOCK])
+    plain[...] = jnp.concatenate(held, axis=0).astype(bf16)
+    out[:, :width] = jnp.concatenate(normed, axis=0).astype(bf16)
+    out[:, width:] = jnp.concatenate(metas, axis=0).astype(bf16)
+
+
+def select_kernel(step, place, b0, b1, b2, b3, o0, o1, o2, o3, weights):
+    mine = slice(step * BLOCK, (step + 1) * BLOCK)
+    held = jnp.concatenate([b[...].astype(f32)[mine] for b in (b0, b1, b2, b3)], axis=0)
     width = held.shape[1] - META
     half = width // 2
+    many = SIDE * 2 * PART
+    count = SIDE * BLOCK
     meta = held[:, width:]
-    lane = lax.broadcasted_iota(jnp.int32, meta.shape, 1)
-    named = jnp.where((meta > 0) & (lane < EXPERTS), 1.0, 0.0).astype(bf16)
+    named = jnp.where((meta > 0) & (row_of(meta.shape, 1) < EXPERTS), 1.0, 0.0).astype(bf16)
     meta = meta.astype(bf16)
-    before = dot(lower[...], named).astype(bf16)
-    here = (dot(pick[0], named, NT) > 0.5) & (dot(pick[0], before, NT) == fixed[1]) & (fixed[0] > 0.5)
-    second = fixed[2] > 0.5
+    later, sooner = row_of((count, count), 0), row_of((count, count), 1)
+    same = digits(later, BLOCK, SIDE)[0] == digits(sooner, BLOCK, SIDE)[0]
+    before = dot(jnp.where(same & (sooner < later), 1.0, 0.0).astype(bf16), named).astype(bf16)
+    block, rest = digits(row_of((many, META), 0), 2 * PART, SIDE)
+    z = place[1] + block
+    expert = place[0] * SIDE + jnp.where(z >= SIDE, z - SIDE, z)
+    lane = row_of((many, META), 1)
+    pick_high = jnp.where(lane == expert, 1.0, 0.0).astype(bf16)
+    pick_low = jnp.where(lane == expert + EXPERTS, 1.0, 0.0).astype(bf16)
+    _, rest = digits(row_of((many, count), 0), 2 * PART, SIDE)
+    second, slot = digits(rest, PART, 2)
+    source, turn = digits(slot, CAP, SIDE)
+    owner = digits(row_of((many, count), 1), BLOCK, SIDE)[0]
+    here = (
+        (dot(pick_high, named, NT) > 0.5)
+        & (dot(pick_high, before, NT) == turn.astype(f32))
+        & (source == owner)
+    )
     sel = jnp.where(here, 1.0, 0.0)
-    low_half = jnp.where(second, 0.0, sel).astype(bf16)
-    high_half = jnp.where(second, sel, 0.0).astype(bf16)
-    weights[0] = jnp.where(here, dot(pick[0], meta, NT), 0.0)
-    weights[1] = jnp.where(here, dot(pick[1], meta, NT), 0.0)
+    low_half = jnp.where(second > 0, 0.0, sel).astype(bf16)
+    high_half = jnp.where(second > 0, sel, 0.0).astype(bf16)
+    weights[0] = jnp.where(here, dot(pick_high, meta, NT), 0.0)
+    weights[1] = jnp.where(here, dot(pick_low, meta, NT), 0.0)
     slots = dot(low_half, held[:, :half].astype(bf16)) + dot(high_half, held[:, half:width].astype(bf16))
     for i, o in enumerate((o0, o1, o2, o3)):
         o[...] = slots[i * 2 * PART : (i + 1) * 2 * PART].astype(bf16)
 
 
-def assemble_kernel(place, f0, f1, f2, f3, out):
+def assemble_kernel(f0, f1, f2, f3, out):
     half = f0.shape[1]
     for h in range(2):
         total = 0.0
         for i, f in enumerate((f0, f1, f2, f3)):
-            total = total + dot(place[h, i], f[...])
+            total = total + dot(placed(h, i), f[...])
         out[:, h * half : (h + 1) * half] = total.astype(bf16)
 
 
-def finish_kernel(place, own, plus, minus, la, rb, o0, o1, o2, o3):
+def finish_kernel(own, plus, minus, la, rb, o0, o1, o2, o3):
     quarter = la.shape[0]
     half = own.shape[1] // 2
     total = [0.0] * SIDE
@@ -138,7 +169,7 @@
         second = mine[quarter:] + plus[:, cols].astype(f32)[:quarter] + rb[:, cols].astype(f32)
         summed = jnp.concatenate([first, second], axis=0).astype(bf16)
         for i in range(SIDE):
-            total[i] = total[i] + dot(place[h, i], summed, TN)
+            total[i] = total[i] + dot(placed(h, i), summed, TN)
     for i, o in enumerate((o0, o1, o2, o3)):
         o[...] = total[i].astype(bf16)
 
@@ -148,10 +179,10 @@
     quarter = lb.shape[0]
     piece = [total[i * quarter : (i + 1) * quarter] for i in range(8)]
     own[...] = total[: 2 * quarter].astype(bf16)
-    lb[...] = piece[2].astype(bf16)
-    ra[...] = piece[3].astype(bf16)
-    plus[...] = jnp.concatenate([piece[4], piece[6]], axis=0).astype(bf16)
-    minus[...] = jnp.concatenate([piece[5], piece[7]], axis=0).astype(bf16)
+    lb[...] = piece[3].astype(bf16)
+    ra[...] = piece[4].astype(bf16)
+    plus[...] = jnp.concatenate([piece[5], piece[6]], axis=0).astype(bf16)
+    minus[...] = jnp.concatenate([piece[2], piece[7]], axis=0).astype(bf16)
 
 
 def pair_sums(kept, got):
@@ -164,26 +195,37 @@
         out_shape=[jax.ShapeDtypeStruct((r, width), bf16) for r in rows],
         in_specs=[pl.BlockSpec((many, chunk), lambda s: (0, s))] * 2,
         out_specs=[pl.BlockSpec((r, chunk), lambda s: (0, s)) for r in rows],
-        compiler_params=pltpu.CompilerParams(vmem_limit_bytes=24 * 2**20),
+        compiler_params=pltpu.CompilerParams(vmem_limit_bytes=16 * 2**20),
         cost_estimate=pl.CostEstimate(flops=many * width, bytes_accessed=6 * many * width, transcendentals=0),
     )(kept, got)
 
 
-def combine_kernel(fixed, weights, f0, f1, f2, f3, own, o1, o2, o3):
+def weighted(weights, parts, h):
+    second = row_of((2 * PART, SIDE * BLOCK), 0) >= PART
+    mine = second if h else jnp.logical_not(second)
+    total = 0.0
+    for i in range(SIDE):
+        rows = slice(i * 2 * PART, (i + 1) * 2 * PART)
+        for k in range(2):
+            share = jnp.where(mine, weights[k, rows], 0.0).astype(bf16)
+            total = total + dot(share, parts[i][...], TN)
+    return total
+
+
+def gather_kernel(weights, f0, f1, f2, f3, out):
     half = f0.shape[1]
-    many = 2 * PART
+    for h in range(2):
+        out[:, h * half : (h + 1) * half] = weighted(weights, (f0, f1, f2, f3), h)
+
+
+def combine_kernel(before, weights, f0, f1, f2, f3, own, o1, o2, o3):
+    half = f0.shape[1]
     for h in range(2):
         cols = slice(h * half, (h + 1) * half)
-        total = 0.0
-        for i, f in enumerate((f0, f1, f2, f3)):
-            rows = slice(i * many, (i + 1) * many)
-            mine = (fixed[2, rows] > 0.5) if h else (fixed[2, rows] < 0.5)
-            for k in range(2):
-                share = jnp.where(mine, weights[k, rows], 0.0).astype(bf16)
-                total = total + dot(share, f[...], TN)
-        own[:, cols] = total[:BLOCK]
-        for i, o in enumerate((o1, o2, o3)):
-            o[:, cols] = total[(i + 1) * BLOCK : (i + 2) * BLOCK].astype(bf16)
+        total = weighted(weights, (f0, f1, f2, f3), h)
+        for i, o in enumerate((own, o1, o2, o3)):
+            rows = slice(i * BLOCK, (i + 1) * BLOCK)
+            o[:, cols] = jnp.concatenate([before[rows, cols], total[rows]], axis=0).astype(o.dtype)
 
 
 CHUNK = 1024
@@ -248,7 +290,7 @@
             pltpu.VMEM((2 * many, units), f32),
             pltpu.VMEM((2 * many, units), bf16),
         ],
-        compiler_params=pltpu.CompilerParams(vmem_limit_bytes=32 * 2**20),
+        compiler_params=pltpu.CompilerParams(vmem_limit_bytes=20 * 2**20),
         cost_estimate=pl.CostEstimate(
             flops=12 * many * width * units, bytes_accessed=6 * width * units + 8 * many * width, transcendentals=0
         ),
@@ -295,7 +337,7 @@
             jax.ShapeDtypeStruct((count, steps, heads, 1), f32),
             jax.ShapeDtypeStruct((count, steps, heads, 1), f32),
         ],
-        compiler_params=pltpu.CompilerParams(vmem_limit_bytes=32 * 2**20),
+        compiler_params=pltpu.CompilerParams(vmem_limit_bytes=12 * 2**20),
         cost_estimate=pl.CostEstimate(
             flops=2 * count * steps * heads * context * (width + LAT),
             bytes_accessed=count * (2 * width * (context + steps * heads) + 4 * steps * heads * LAT),
@@ -366,16 +408,13 @@
         out_specs=pl.BlockSpec((1, tall, 128), lambda r: (r, 0, 0)),
         out_shape=jax.ShapeDtypeStruct((rows, tall, 128), bf16),
         scratch_shapes=[pltpu.VMEM((tall, 128), f32)],
-        compiler_params=pltpu.CompilerParams(vmem_limit_bytes=32 * 2**20),
+        compiler_params=pltpu.CompilerParams(vmem_limit_bytes=12 * 2**20),
     )(queries, new_keys, *first, *last)
 
 
-def project_kernel(core, hidden, own0, a0, b0, c0, own1, a1, b1, c1, gain, kv_own, kv_other, kv_gain, turns, layer, keys, stage):
-    rows = []
-    for t, (own, a, b, c) in enumerate(((own0, a0, b0, c0), (own1, a1, b1, c1))):
-        mixture = own[...] + a[...].astype(f32) + b[...].astype(f32) + c[...].astype(f32)
-        rows.append(hidden[t].astype(f32) + mixture)
-    both = jnp.concatenate(rows, axis=0).astype(bf16)
+def project_kernel(core, hidden, own, a, b, c, gain, kv_own, kv_other, kv_gain, turns, layer, keys, stage):
+    mixture = own[...] + a[...].astype(f32) + b[...].astype(f32) + c[...].astype(f32)
+    both = (hidden[...].astype(f32) + mixture).astype(bf16)
     many, width = both.shape
     wide = both.astype(f32)
     for k in range(width // 128):
@@ -405,13 +444,17 @@
     return [mine, shift(mine, "y", 1), shift(mine, "y", 3), shift(mine, "y", 2)]
 
 
+def ring_x(own):
+    return shift(own, "x", 1), shift(own, "x", 3)
+
+
+def far_x(left, right):
+    half = left.shape[0] // 2
+    return [shift(left[:half], "x", 1), shift(right[half:], "x", 3)]
+
+
 def steps_z(parts, sign):
     return [parts[0]] + [shift(parts[i], "z", sign * i % SIDE) for i in (1, 2, 3)]
-
-
-def near_rows(own, left, right):
-    half = own.shape[0] // 2
-    return jnp.concatenate([own, left[half:], right[:half], right[half:], left[:half]], axis=0)
 
 
 CHIPS = ("y", "z", "x")
@@ -433,19 +476,72 @@
     return whole.swapaxes(1, 2).reshape(width, context)
 
 
-def fresh_sort(here, there, fresh_order):
-    core = lax.axis_index("c")
+def around(value):
+    return jnp.where(value < 0, value + SIDE, jnp.where(value >= SIDE, value - SIDE, value))
+
+
+def pack_kernel(place, cut, *outs):
+    for kx in range(SIDE):
+        for ky in range(SIDE):
+            for kz in range(SIDE):
+                y, z, x = around(place[0] + ky), around(place[1] + kz), around(place[2] + kx)
+                outs[kx][ky * SIDE + kz] = cut[(y * SIDE + z) * SIDE + x]
+
+
+def regroup_kernel(last, *refs):
+    ins, outs = refs[:SIDE], refs[SIDE:]
+    for a in range(SIDE):
+        for b in range(SIDE):
+            for c in range(SIDE):
+                if last:
+                    outs[c][b * SIDE + a] = ins[a][b * SIDE + c]
+                else:
+                    outs[b][a * SIDE + c] = ins[a][b * SIDE + c]
+
+
+def sort_kernel(order, place, here, there, *outs):
     count = here.shape[0]
-    wanted = lax.dynamic_slice_in_dim(fresh_order, core * count, count, 0)
-    own_core = (wanted >= count) == (core > 0)
-    index = wanted % count
-    return jnp.where(
-        own_core[:, None, None], jnp.take(here, index, axis=0), jnp.take(there, index, axis=0)
-    )
-
-
-def to_chips(pieces):
-    return lax.all_to_all(pieces, CHIPS, split_axis=0, concat_axis=0, tiled=True)
+    for jz in range(SIDE):
+        for jy in range(SIDE):
+            for jx in range(SIDE):
+                y, z, x = around(place[0] + jy), around(place[1] + jz), around(place[2] + jx)
+                wanted = order[place[3] * count + (y * SIDE + z) * SIDE + x]
+                upper = wanted >= count
+                source = jnp.where(upper, wanted - count, wanted)
+                sy, sz, sx = source >> 4, (source >> 2) & 3, source & 3
+                kx, ky, kz = around(place[2] - sx), around(place[0] - sy), around(place[1] - sz)
+                index = (kz * SIDE + kx) * SIDE + ky
+                other = jnp.where(upper, 1, 0) != place[3]
+                out = outs[jz].at[jy * SIDE + jx]
+
+                @pl.when(other)
+                def _(out=out, index=index):
+                    out[...] = there[index]
+
+                @pl.when(jnp.logical_not(other))
+                def _(out=out, index=index):
+                    out[...] = here[index]
+
+
+def unpack_kernel(place, x0, x1, x2, x3, whole):
+    for jx, part in enumerate((x0, x1, x2, x3)):
+        for jz in range(SIDE):
+            for jy in range(SIDE):
+                y, z, x = around(place[0] - jy), around(place[1] - jz), around(place[2] - jx)
+                whole[(y * SIDE + z) * SIDE + x] = part[jz * SIDE + jy]
+
+
+def quarters(kernel, *args, smem=0):
+    rows, lanes = args[-1].shape[1:]
+    return call(kernel, [((SIDE * SIDE, rows, lanes), bf16)] * SIDE, *args, smem=smem)
+
+
+def regroup(last, parts):
+    return quarters(functools.partial(regroup_kernel, last), *parts)
+
+
+def stage(parts, axis):
+    return [parts[0], *[shift(parts[i], axis, i) for i in (1, 2, 3)]]
 
 
 def shards(
@@ -470,137 +566,126 @@
     score_scale = (NOPE + ROPE) ** (-0.5)
     core = lax.axis_index("c").astype(jnp.int32).reshape(1)
 
-    shares = route_weight / jnp.sum(route_weight, axis=-1, keepdims=True) * route_scaling
-    dense_share = jnp.sum(
-        jnp.where(
-            expert_ids[..., None] == jnp.arange(EXPERTS, dtype=jnp.int32), shares[..., None], 0.0
-        ),
-        axis=2,
-    )
-    high = dense_share.astype(bf16)
-    low = (dense_share - high.astype(f32)).astype(bf16)
-    normed = rms_scale(hidden_in, ffn_gain).astype(bf16)
-    meta_rows = jnp.concatenate(
-        [high, low, jnp.zeros((steps_count, local_rows, META - 2 * EXPERTS), bf16)], axis=2
-    )
-    payload = jnp.pad(
-        jnp.concatenate([normed, meta_rows], axis=2), ((0, 0), (0, BLOCK - local_rows), (0, 0))
-    )
-    hidden_rows = jnp.pad(hidden_in, ((0, 0), (0, BLOCK - local_rows), (0, 0)))
-
-    pick, fixed, lower = fold_tables()
-    place = jnp.asarray(
-        PLACE.reshape(2, SLOTS, SIDE, 2 * PART).transpose(0, 2, 1, 3), bf16
-    )
+    payload, hidden_rows = call(
+        prepare_kernel,
+        [((steps_count * BLOCK, model_width + META), bf16), ((steps_count * BLOCK, model_width), bf16)],
+        expert_ids.swapaxes(1, 2), route_weight.swapaxes(1, 2), hidden_in.swapaxes(0, 1), ffn_gain[None],
+    )
+
+    position = jnp.stack([lax.axis_index(axis) for axis in ("y", "z", "x", "c")]).astype(jnp.int32)
     folded = ((2 * PART, model_width // 2), bf16)
     query_t = queries.swapaxes(2, 3)
     resident_t = resident_cache.swapaxes(1, 2)
 
     slot_half = SLOTS // 2
-    rows = (BLOCK, model_width)
-
-    def select(held):
+    rows = (steps_count * BLOCK, model_width)
+
+    def select(step, held):
         *parts, weight = call(
-            select_kernel, [folded] * SIDE + [((2, SIDE * 2 * PART, SIDE * BLOCK), f32)],
-            pick, fixed, lower, *held,
+            functools.partial(select_kernel, step), [folded] * SIDE + [((2, SIDE * 2 * PART, SIDE * BLOCK), f32)],
+            position, *held, smem=1,
         )
         return parts, weight
 
     def assemble(parts):
-        return call(assemble_kernel, [((SLOTS, model_width), bf16)], place, *parts)[0]
-
-    def combine(weight, parts):
-        return call(
-            combine_kernel, [(rows, f32), (rows, bf16), (rows, bf16), (rows, bf16)],
-            fixed, weight, *parts,
-        )
+        return call(assemble_kernel, [((SLOTS, model_width), bf16)], *parts)[0]
+
+    def combine(*args):
+        return call(combine_kernel, [(rows, f32), (rows, bf16), (rows, bf16), (rows, bf16)], *args)
+
+    def gather_slots(weight, parts):
+        return call(gather_kernel, [((SIDE * BLOCK, model_width), f32)], weight, *parts)[0]
 
     def back_y(own, one, two, three):
         return [own, shift(one, "y", 3), shift(two, "y", 1), shift(three, "y", 2)]
 
     def finish(own, plus, minus, la, rb):
-        return call(finish_kernel, [folded] * SIDE, place, own, plus, minus, la, rb)
-
-    def run_experts(near, near_swapped, far, far_swapped):
-        return experts([near, far], [near_swapped, far_swapped], expert_gate, expert_up, expert_down)
+        return call(finish_kernel, [folded] * SIDE, own, plus, minus, la, rb)
+
+    def run_experts(pieces, swapped):
+        return experts(list(pieces), list(swapped), expert_gate, expert_up, expert_down)
 
     def meet(ra, lb, plus, minus):
         return add(ra, plus[slot_half:]), add(lb, minus[slot_half:])
 
-    held = steps_y(payload[0])
-    pieces = fresh_cut(fresh_cache[0].T)
-    held, payload1, pieces = hold(held, payload[1], pieces)
-    parts, weight0 = select(held)
+    held = steps_y(payload)
+    moving = stage(quarters(pack_kernel, position, fresh_cut(fresh_cache[0].T), smem=1), "x")
+    held, moving = hold(held, moving)
+    parts, weight0 = select(0, held)
     parts = steps_z(parts, 1)
-    held = steps_y(payload1)
-    here = to_chips(pieces)
-    parts, held, weight0, here = hold(parts, held, weight0, here)
-    own0 = assemble(parts)
-    left0, right0 = shift(own0, "x", 1), shift(own0, "x", 3)
-    parts, weight1 = select(held)
-    parts = steps_z(parts, 1)
-    there = swap(here)
-    past_resident = past(cache_len, query_t, resident_t, score_scale, 0)
-    own0, left0, right0, parts, weight1, here, there, past_resident = hold(
-        own0, left0, right0, parts, weight1, here, there, past_resident
-    )
-    far_a, far_b = shift(left0[:slot_half], "x", 1), shift(right0[slot_half:], "x", 3)
-    near0 = near_rows(own0, left0, right0)
-    near0_swapped = swap(near0)
+    parts1, weight1 = select(1, held)
+    moving = stage(regroup(False, moving), "y")
+    parts, weight0, parts1, weight1, moving = hold(parts, weight0, parts1, weight1, moving)
+    own = assemble(parts)
+    near = ring_x(own)
+    parts = steps_z(parts1, 1)
+    moving = regroup(True, moving)
+    own, near, parts, moving = hold(own, near, parts, moving)
+    far = far_x(*near)
+    around_own = jnp.concatenate([own, *near], axis=0)
+    near_swapped = swap(around_own)
     own1 = assemble(parts)
-    sorted_pieces = fresh_sort(here, there, fresh_order)
-    far_a, far_b, near0, near0_swapped, own1, sorted_pieces = hold(
-        far_a, far_b, near0, near0_swapped, own1, sorted_pieces
-    )
-    left1, right1 = shift(own1, "x", 1), shift(own1, "x", 3)
-    far0 = jnp.concatenate([far_a, far_b], axis=0)
-    kept0, sent0 = run_experts(near0, near0_swapped, far0, swap(far0))
-    left1, right1, kept0, sent0, sorted_pieces = hold(left1, right1, kept0, sent0, sorted_pieces)
-    far_a, far_b = shift(left1[:slot_half], "x", 1), shift(right1[slot_half:], "x", 3)
+    around_own, far, near_swapped, own1, moving = hold(around_own, far, near_swapped, own1, moving)
+    moving = stage(moving, "z")
+    near1 = ring_x(own1)
+    far_swapped = [swap(piece) for piece in far]
+    kept0, sent0 = run_experts([around_own, *far], [near_swapped, *far_swapped])
+    own1, near1, kept0, sent0, moving = hold(own1, near1, kept0, sent0, moving)
+    far = far_x(*near1)
     got0 = swap(sent0)
-    near1 = near_rows(own1, left1, right1)
-    near1_swapped = swap(near1)
+    around_own = jnp.concatenate([own1, *near1], axis=0)
+    near_swapped = swap(around_own)
     own0, lb0, ra0, plus0, minus0 = pair_sums(kept0, got0)
-    far_a, far_b, near1, near1_swapped, own0, lb0, ra0, plus0, minus0, sorted_pieces = hold(
-        far_a, far_b, near1, near1_swapped, own0, lb0, ra0, plus0, minus0, sorted_pieces
+    here = jnp.concatenate(moving, axis=0)
+    moving = [here, swap(here)]
+    far, near_swapped, around_own, own0, lb0, ra0, plus0, minus0, moving = hold(
+        far, near_swapped, around_own, own0, lb0, ra0, plus0, minus0, moving
     )
     plus0, minus0 = shift(plus0, "x", 1), shift(minus0, "x", 3)
-    far1 = jnp.concatenate([far_a, far_b], axis=0)
-    kept1, sent1 = run_experts(near1, near1_swapped, far1, swap(far1))
-    plus0, minus0, kept1, sent1, sorted_pieces = hold(plus0, minus0, kept1, sent1, sorted_pieces)
+    far_swapped = [swap(piece) for piece in far]
+    kept1, sent1 = run_experts([around_own, *far], [near_swapped, *far_swapped])
+    moving = quarters(sort_kernel, fresh_order, position, *moving, smem=2)
+    plus0, minus0, kept1, sent1, moving = hold(plus0, minus0, kept1, sent1, moving)
     ra0, lb0 = meet(ra0, lb0, plus0, minus0)
     la0, rb0 = shift(ra0, "x", 1), shift(lb0, "x", 3)
     got1 = swap(sent1)
     own1, lb1, ra1, plus1, minus1 = pair_sums(kept1, got1)
-    la0, rb0, own1, lb1, ra1, plus1, minus1, sorted_pieces = hold(
-        la0, rb0, own1, lb1, ra1, plus1, minus1, sorted_pieces
-    )
+    moving = regroup(False, stage(moving, "z"))
+    la0, rb0, own1, lb1, ra1, plus1, minus1, moving = hold(
+        la0, rb0, own1, lb1, ra1, plus1, minus1, moving
+    )
+    other_down = swap(kv_down.T)
     plus1, minus1 = shift(plus1, "x", 1), shift(minus1, "x", 3)
     parts = steps_z(finish(own0, plus0, minus0, la0, rb0), -1)
-    whole = to_chips(sorted_pieces)
-    plus1, minus1, parts, whole = hold(plus1, minus1, parts, whole)
+    past_resident = past(cache_len, query_t, resident_t, score_scale, 0)
+    plus1, minus1, parts0, moving, past_resident, other_down = hold(
+        plus1, minus1, parts, moving, past_resident, other_down
+    )
     ra1, lb1 = meet(ra1, lb1, plus1, minus1)
     la1, rb1 = shift(ra1, "x", 1), shift(lb1, "x", 3)
-    mixed0 = back_y(*combine(weight0, parts))
+    moving = regroup(True, stage(moving, "y"))
+    total0 = gather_slots(weight0, parts0)
+    la1, rb1, moving, total0 = hold(la1, rb1, moving, total0)
+    parts = steps_z(finish(own1, plus1, minus1, la1, rb1), -1)
+    moving = stage(moving, "x")
+    parts, moving = hold(parts, moving)
+    mixed = back_y(*combine(total0, weight1, *parts))
+    (whole,) = call(unpack_kernel, [((SIDE**3, *moving[0].shape[1:]), bf16)], position, *moving, smem=1)
     fresh_t = fresh_join(whole, LAT + ROPE, fresh_cache.shape[1])[None]
     past_fresh = past(cache_len[resident_rows:], query_t, fresh_t, score_scale, resident_rows)
-    la1, rb1, mixed0, past_fresh = hold(la1, rb1, mixed0, past_fresh)
-    parts = steps_z(finish(own1, plus1, minus1, la1, rb1), -1)
-    other_down = swap(kv_down.T)
-    mixed = mixed0 + back_y(*combine(weight1, parts))
-
-    positions = jnp.pad(cache_len, (0, BLOCK - local_rows)).astype(f32)[None, :]
-    positions = (positions + jnp.arange(steps_count).astype(f32)[:, None]).reshape(-1)
-    halfway = ROPE // 2
-    frequency = rope_base ** (-2.0 * jnp.arange(halfway).astype(f32) / ROPE)
-    angles = positions[:, None] * frequency[None, :]
-    turns = jnp.stack([jnp.tile(jnp.cos(angles), (1, 2)), jnp.tile(jnp.sin(angles), (1, 2))])
+    mixed, past_fresh = hold(mixed, past_fresh)
+
+    positions = jnp.pad(cache_len, (0, BLOCK - local_rows)).astype(f32)
+    positions = (positions[None, :] + jnp.arange(steps_count).astype(f32)[:, None]).reshape(-1, 1)
+    frequency = (rope_base ** (-2.0 * np.arange(ROPE // 2) / ROPE)).astype(np.float32)
+    angles = positions * jnp.asarray(np.tile(frequency, 2))[None, :]
+    turns = jnp.stack([jnp.cos(angles), jnp.sin(angles)])
     many = steps_count * BLOCK
     layer, keys = call(
         project_kernel,
         [((many * model_width // 128, 128), bf16), ((many, LAT + ROPE), bf16)],
         core, hidden_rows, *mixed, attn_gain[None], kv_down.T, other_down, kv_gain[None], turns,
-        smem=1, limit=40, scratch=[pltpu.VMEM((many * model_width // 128, 128), f32)],
+        smem=1, limit=18, scratch=[pltpu.VMEM((many * model_width // 128, 128), f32)],
     )
     tall = model_width // 128
     layer = layer[: local_rows * steps_count * tall].reshape(local_rows, tall, steps_count, 128)

time: 259 us -> 213 us (0.82)
  local copies, waits for them, and re-layouts: 57.7 us -> 14.9 us
  other arithmetic: 9.84 us -> 1.85 us
  waiting for transfers between devices: 54.3 us -> 58.2 us
    unnamed x134 -> x69, local copies, waits for them, and re-layouts: 43.2 us -> 10.2 us
    all_to_all x2 -> x0, starting transfers between devices: 18.1 us -> none  [to_chips(): lax.all_to_all(pieces, CHIPS, split_axis=0, concat_axis=0, tiled=True)]
    ppermute x48 -> x62, starting transfers between devices: 64.1 us -> 81.8 us  [shift(): lax.ppermute(values, axis, [(i, (i + by) % size) for i in range(size)])]
    gather x2 -> x0, local copies, waits for them, and re-layouts: 5.16 us -> none  [the longest x1 2.59 us: fresh_sort(): jnp.take(here, index, axis=0)]
    pallas_call x9 -> x17, Pallas kernels: 14.4 us -> 18.4 us  [call(): pl.pallas_call(kernel, out_shape=[jax.ShapeDtypeStruct(shape, dtype) for...]
    ppermute x48 -> x62, waiting for transfers between devices: 54.3 us -> 58.2 us  [shift(): lax.ppermute(values, axis, [(i, (i + by) % size) for i in range(size)])]
  transfers between devices with their start and end apart: 50 -> 62, of which waited for: 20 -> 22; matrix products, arithmetic and copies ran while one was open for 7% -> 2% of each run, Pallas kernels for 16% -> 19%
where the time goes in v2:
time: 213 us; the launch traced here: 211 us
  starting transfers between devices  81.8 us (38%)
  waiting for transfers between devices  58.2 us (27%)
  Pallas kernels  52.9 us (25%)
  local copies, waits for them, and re-layouts  14.9 us (7%)
    ppermute x62, starting transfers between devices, shift(): lax.ppermute(values, axis, [(i, (i + by) % size) for i in range(size)])  81.8 us
    ppermute x62, waiting for transfers between devices, shift(): lax.ppermute(values, axis, [(i, (i + by) % size) for i in range(size)])  58.2 us
    pallas_call x17, Pallas kernels, call(): pl.pallas_call(kernel, out_shape=[jax.ShapeDtypeStruct(shape, dtype) for...  18.4 us
    pallas_call x2, Pallas kernels, experts(): pl.pallas_call(functools.partial(expert_kernel, pieces, chunks), grid=(2...  17.5 us
    unnamed x69, local copies, waits for them, and re-layouts  10.2 us
    pallas_call x2, Pallas kernels, past(): pl.pallas_call(functools.partial(past_kernel, scale), grid_spec=pltpu.Pre...  8.55 us
    pallas_call x1, Pallas kernels, merge(): pl.pallas_call(functools.partial(merge_kernel, scale, count), grid=(rows,...  5.78 us
  transfers between devices with their start and end apart: 62, of which 22 were waited for; matrix products, arithmetic and copies ran while one was open for 2% of the time, Pallas kernels for 19%

profile of v2, /device:TPU:0, one launch (start us, length us, event | category | flops | bytes accessed | tf_op | source)
XLA Modules:
  0.0 211.0 jit_solution(2466292712630767624)
XLA Ops:
  12.1 2.7 %collective-permute-start.4 = (bf16[16,40,128]{2,1,0:T(8,128)(2,1)S(1)}, bf16[16,40,128]{2,1,0:T(8,128)(2,1)S(1)}, u32[]{:S(2)}, u32[]{:S(2)}) collective-permute-start(bf16[16,40,128]{2,1,0:T(8,128)(2,1)S(1)} %get-tuple-element.193), channel_id=1, source_target_pairs={{0,2},{1,3},{2,0},{3,1},{4,6},{5,7},{6,4},{7,5},{8,10},{9,11},{10,... | collective-permute-start | bytes 491528 | tf_op jit(solution)/shard_map/ppermute | solution.py:44
  16.3 2.7 %collective-permute-done.4.refs_2_ = bf16[16,40,128]{2,1,0:T(8,128)(2,1)S(1)} collective-permute-done((bf16[16,40,128]{2,1,0:T(8,128)(2,1)S(1)}, bf16[16,40,128]{2,1,0:T(8,128)(2,1)S(1)}, u32[]{:S(2)}, u32[]{:S(2)}) %collective-permute-start.4) | collective-permute-done | bytes 163872 | tf_op jit(solution)/shard_map/ppermute | solution.py:44
  18.9 2.2 %collective-permute-done.5.refs_3_ = bf16[16,40,128]{2,1,0:T(8,128)(2,1)S(1)} collective-permute-done((bf16[16,40,128]{2,1,0:T(8,128)(2,1)S(1)}, bf16[16,40,128]{2,1,0:T(8,128)(2,1)S(1)}, u32[]{:S(2)}, u32[]{:S(2)}) %collective-permute-start.5) | collective-permute-done | bytes 163872 | tf_op jit(solution)/shard_map/ppermute | solution.py:44
  26.3 3.6 %collective-permute-start.7 = (bf16[24,3584]{1,0:T(8,128)(2,1)S(1)}, bf16[24,3584]{1,0:T(8,128)(2,1)S(1)}, u32[]{:S(2)}, u32[]{:S(2)}) collective-permute-start(bf16[24,3584]{1,0:T(8,128)(2,1)S(1)} %get-tuple-element.201), channel_id=1, source_target_pairs={{0,8},{4,12},{8,0},{12,4},{1,9},{5,13},{9,1},{13,5},{2,10},{6,14},... | collective-permute-start | bytes 516104 | tf_op jit(solution)/shard_map/ppermute | solution.py:44
  30.9 2.5 %collective-permute-start.11 = (bf16[16,40,128]{2,1,0:T(8,128)(2,1)S(1)}, bf16[16,40,128]{2,1,0:T(8,128)(2,1)S(1)}, u32[]{:S(2)}, u32[]{:S(2)}) collective-permute-start(bf16[16,40,128]{2,1,0:T(8,128)(2,1)S(1)} %get-tuple-element.216), channel_id=1, source_target_pairs={{0,48},{16,0},{32,16},{48,32},{1,49},{17,1},{33,17},{49,33},{2,50}... | collective-permute-start | bytes 491528 | tf_op jit(solution)/shard_map/ppermute | solution.py:44
  36.2 3.7 %collective-permute-done.9.refs_1_ = bf16[16,40,128]{2,1,0:T(8,128)(2,1)S(1)} collective-permute-done((bf16[16,40,128]{2,1,0:T(8,128)(2,1)S(1)}, bf16[16,40,128]{2,1,0:T(8,128)(2,1)S(1)}, u32[]{:S(2)}, u32[]{:S(2)}) %collective-permute-start.9) | collective-permute-done | bytes 163872 | tf_op jit(solution)/shard_map/ppermute | solution.py:44
  45.5 2.2 %collective-permute-start.16 = (bf16[24,3584]{1,0:T(8,128)(2,1)S(1)}, bf16[24,3584]{1,0:T(8,128)(2,1)S(1)}, u32[]{:S(2)}, u32[]{:S(2)}) collective-permute-start(bf16[24,3584]{1,0:T(8,128)(2,1)S(1)} %get-tuple-element.224), channel_id=1, source_target_pairs={{0,12},{4,0},{8,4},{12,8},{1,13},{5,1},{9,5},{13,9},{2,14},{6,2},{... | collective-permute-start | bytes 516104 | tf_op jit(solution)/shard_map/ppermute | solution.py:44
  47.8 4.7 %collective-permute-done.14.f1 = bf16[24,3584]{1,0:T(8,128)(2,1)S(1)} collective-permute-done((bf16[24,3584]{1,0:T(8,128)(2,1)S(1)}, bf16[24,3584]{1,0:T(8,128)(2,1)S(1)}, u32[]{:S(2)}, u32[]{:S(2)}) %collective-permute-start.14) | collective-permute-done | bytes 172064 | tf_op jit(solution)/shard_map/ppermute | solution.py:44
  57.0 2.4 %collective-permute-start.18 = (bf16[24,7168]{1,0:T(8,128)(2,1)S(1)}, bf16[24,7168]{1,0:T(8,128)(2,1)S(1)}, u32[]{:S(2)}, u32[]{:S(2)}) collective-permute-start(bf16[24,7168]{1,0:T(8,128)(2,1)S(1)} %slice.34), channel_id=1, source_target_pairs={{0,3},{1,0},{2,1},{3,2},{4,7},{5,4},{6,5},{7,6},{8,11},{9,8},{10,9... | collective-permute-start | bytes 1032200 | tf_op jit(solution)/shard_map/ppermute | solution.py:44
  60.2 7.6 %collective-permute-done.17.refs_1_ = bf16[24,7168]{1,0:T(8,128)(2,1)S(1)} collective-permute-done((bf16[24,7168]{1,0:T(8,128)(2,1)S(1)}, bf16[24,7168]{1,0:T(8,128)(2,1)S(1)}, u32[]{:S(2)}, u32[]{:S(2)}) %collective-permute-start.17) | collective-permute-done | bytes 344096 | tf_op jit(solution)/shard_map/ppermute | solution.py:44
  69.0 2.5 %collective-permute-start.21 = (bf16[48,7168]{1,0:T(8,128)(2,1)S(1)}, bf16[48,7168]{1,0:T(8,128)(2,1)S(1)}, u32[]{:S(2)}, u32[]{:S(2)}) collective-permute-start(bf16[48,7168]{1,0:T(8,128)(2,1)S(1)} %shard_map.174), channel_id=1, source_target_pairs={{0,3},{1,0},{2,1},{3,2},{4,7},{5,4},{6,5},{7,6},{8,11},{9,8},{10,9... | collective-permute-start | bytes 2064392 | tf_op jit(solution)/shard_map/ppermute | solution.py:44
  75.7 8.7 %shard_map.175 = (bf16[192,7168]{1,0:T(8,128)(2,1)S(1)}, bf16[192,7168]{1,0:T(8,128)(2,1)S(1)}) custom-call(bf16[144,7168]{1,0:T(8,128)(2,1)S(1)} %constant_dynamic-update-slice_fusion.refs_0_, bf16[24,7168]{1,0:T(8,128)(2,1)S(1)} %collective-permute-done.17.refs_1_, bf16[24,7168]{1,0:T(8,128)(2,1)S(1)} %collective-permute-done.18.refs_2_, ...), custom_call_target="tpu_custom_call" | custom-call | flops 4227858432 | bytes 22020096 | tf_op jit(solution)/shard_map/pallas_call | solution.py:281
  84.5 2.4 %collective-permute-done.20 = bf16[48,7168]{1,0:T(8,128)(2,1)S(1)} collective-permute-done((bf16[48,7168]{1,0:T(8,128)(2,1)S(1)}, bf16[48,7168]{1,0:T(8,128)(2,1)S(1)}, u32[]{:S(2)}, u32[]{:S(2)}) %collective-permute-start.20) | collective-permute-done | bytes 688160 | tf_op jit(solution)/shard_map/ppermute | solution.py:44
  89.1 2.2 %collective-permute-start.28 = (bf16[24,7168]{1,0:T(8,128)(2,1)S(1)}, bf16[24,7168]{1,0:T(8,128)(2,1)S(1)}, u32[]{:S(2)}, u32[]{:S(2)}) collective-permute-start(bf16[24,7168]{1,0:T(8,128)(2,1)S(1)} %slice.36), channel_id=1, source_target_pairs={{0,3},{1,0},{2,1},{3,2},{4,7},{5,4},{6,5},{7,6},{8,11},{9,8},{10,9... | collective-permute-start | bytes 1032200 | tf_op jit(solution)/shard_map/ppermute | solution.py:44
  93.3 6.4 %collective-permute-done.27.refs_1_ = bf16[24,7168]{1,0:T(8,128)(2,1)S(1)} collective-permute-done((bf16[24,7168]{1,0:T(8,128)(2,1)S(1)}, bf16[24,7168]{1,0:T(8,128)(2,1)S(1)}, u32[]{:S(2)}, u32[]{:S(2)}) %collective-permute-start.27) | collective-permute-done | bytes 344096 | tf_op jit(solution)/shard_map/ppermute | solution.py:44
  103.6 2.6 %shard_map.178 = (bf16[16,40,128]{2,1,0:T(8,128)(2,1)S(1)}, bf16[16,40,128]{2,1,0:T(8,128)(2,1)S(1)}, bf16[16,40,128]{2,1,0:T(8,128)(2,1)S(1)}, bf16[16,40,128]{2,1,0:T(8,128)(2,1)S(1)}) custom-call(s32[128]{0:T(128)S(1)} %copy-done.28, s32[4]{0:T(128)S(1)} %pad_add_fusion.place, bf16[64,40,128]{2,1,0:T(8,128)(2,1)S(1)} %constant_dynamic-update-slice_fusion.6.here, ...), custom_call_target="tpu_custom_call" | custom-call | bytes 1311248 | tf_op jit(solution)/shard_map/pallas_call | solution.py:63
  106.2 8.7 %shard_map.177 = (bf16[192,7168]{1,0:T(8,128)(2,1)S(1)}, bf16[192,7168]{1,0:T(8,128)(2,1)S(1)}) custom-call(bf16[144,7168]{1,0:T(8,128)(2,1)S(1)} %constant_dynamic-update-slice_fusion.3.refs_0_, bf16[24,7168]{1,0:T(8,128)(2,1)S(1)} %collective-permute-done.27.refs_1_, bf16[24,7168]{1,0:T(8,128)(2,1)S(1)} %collective-permute-done.28.refs_2_, ...), custom_call_target="tpu_custom_call" | custom-call | flops 4227858432 | bytes 22020096 | tf_op jit(solution)/shard_map/pallas_call | solution.py:281
  114.9 4.0 %collective-permute-done.32.plus = bf16[48,7168]{1,0:T(8,128)(2,1)S(1)} collective-permute-done((bf16[48,7168]{1,0:T(8,128)(2,1)S(1)}, bf16[48,7168]{1,0:T(8,128)(2,1)S(1)}, u32[]{:S(2)}, u32[]{:S(2)}) %collective-permute-start.32) | collective-permute-done | bytes 688160 | tf_op jit(solution)/shard_map/ppermute | solution.py:44
  120.6 3.0 %collective-permute-start.37 = (bf16[24,7168]{1,0:T(8,128)(2,1)S(1)}, bf16[24,7168]{1,0:T(8,128)(2,1)S(1)}, u32[]{:S(2)}, u32[]{:S(2)}) collective-permute-start(bf16[24,7168]{1,0:T(8,128)(2,1)S(1)} %add_convert_fusion.2), channel_id=1, source_target_pairs={{0,3},{1,0},{2,1},{3,2},{4,7},{5,4},{6,5},{7,6},{8,11},{9,8},{10,9... | collective-permute-start | bytes 1032200 | tf_op jit(solution)/shard_map/ppermute | solution.py:44
  126.2 6.2 %collective-permute-done.40.refs_2_ = bf16[16,40,128]{2,1,0:T(8,128)(2,1)S(1)} collective-permute-done((bf16[16,40,128]{2,1,0:T(8,128)(2,1)S(1)}, bf16[16,40,128]{2,1,0:T(8,128)(2,1)S(1)}, u32[]{:S(2)}, u32[]{:S(2)}) %collective-permute-start.40) | collective-permute-done | bytes 163872 | tf_op jit(solution)/shard_map/ppermute | solution.py:44
  133.4 4.3 %collective-permute-done.41.refs_3_ = bf16[16,40,128]{2,1,0:T(8,128)(2,1)S(1)} collective-permute-done((bf16[16,40,128]{2,1,0:T(8,128)(2,1)S(1)}, bf16[16,40,128]{2,1,0:T(8,128)(2,1)S(1)}, u32[]{:S(2)}, u32[]{:S(2)}) %collective-permute-start.41) | collective-permute-done | bytes 163872 | tf_op jit(solution)/shard_map/ppermute | solution.py:44
  143.2 2.5 %collective-permute-start.44 = (bf16[24,3584]{1,0:T(8,128)(2,1)S(1)}, bf16[24,3584]{1,0:T(8,128)(2,1)S(1)}, u32[]{:S(2)}, u32[]{:S(2)}) collective-permute-start(bf16[24,3584]{1,0:T(8,128)(2,1)S(1)} %get-tuple-element.309), channel_id=1, source_target_pairs={{0,12},{4,0},{8,4},{12,8},{1,13},{5,1},{9,5},{13,9},{2,14},{6,2},{... | collective-permute-start | bytes 516104 | tf_op jit(solution)/shard_map/ppermute | solution.py:44
  146.7 6.8 %shard_map.182 = (f32[6,2,128,512]{3,2,1,0:T(8,128)S(1)}, f32[6,2,128,1]{3,2,1,0:T(8,128)S(1)}, f32[6,2,128,1]{3,2,1,0:T(8,128)S(1)}) custom-call(s32[7]{0:T(128)S(1)} %copy-done.30, bf16[2,7,576,128]{3,2,1,0:T(8,128)(2,1)S(1)} %bitcast.43, bf16[6,576,512]{2,1,0:T(8,128)(2,1)S(1)} %bitcast.58), custom_call_target="tpu_custom_call" | custom-call | flops 1711276032 | bytes 8454144 | tf_op jit(solution)/shard_map/pallas_call | solution.py:320
  154.6 3.4 %collective-permute-start.49 = (bf16[24,7168]{1,0:T(8,128)(2,1)S(1)}, bf16[24,7168]{1,0:T(8,128)(2,1)S(1)}, u32[]{:S(2)}, u32[]{:S(2)}) collective-permute-start(bf16[24,7168]{1,0:T(8,128)(2,1)S(1)} %add_convert_fusion), channel_id=1, source_target_pairs={{0,3},{1,0},{2,1},{3,2},{4,7},{5,4},{6,5},{7,6},{8,11},{9,8},{10,9... | collective-permute-start | bytes 1032200 | tf_op jit(solution)/shard_map/ppermute | solution.py:44
  158.3 2.5 %collective-permute-start.51 = (bf16[16,40,128]{2,1,0:T(8,128)(2,1)S(1)}, bf16[16,40,128]{2,1,0:T(8,128)(2,1)S(1)}, u32[]{:S(2)}, u32[]{:S(2)}) collective-permute-start(bf16[16,40,128]{2,1,0:T(8,128)(2,1)S(1)} %get-tuple-element.324), channel_id=1, source_target_pairs={{0,32},{16,48},{32,0},{48,16},{1,33},{17,49},{33,1},{49,17},{2,34}... | collective-permute-start | bytes 491528 | tf_op jit(solution)/shard_map/ppermute | solution.py:44
  164.0 2.6 %collective-permute-done.50.refs_1_ = bf16[16,40,128]{2,1,0:T(8,128)(2,1)S(1)} collective-permute-done((bf16[16,40,128]{2,1,0:T(8,128)(2,1)S(1)}, bf16[16,40,128]{2,1,0:T(8,128)(2,1)S(1)}, u32[]{:S(2)}, u32[]{:S(2)}) %collective-permute-start.50) | collective-permute-done | bytes 163872 | tf_op jit(solution)/shard_map/ppermute | solution.py:44
  173.9 4.1 %collective-permute-start.57 = (bf16[16,40,128]{2,1,0:T(8,128)(2,1)}, bf16[16,40,128]{2,1,0:T(8,128)(2,1)}, u32[]{:S(2)}, u32[]{:S(2)}) collective-permute-start(bf16[16,40,128]{2,1,0:T(8,128)(2,1)} %get-tuple-element.346), channel_id=1, source_target_pairs={{0,2},{1,3},{2,0},{3,1},{4,6},{5,7},{6,4},{7,5},{8,10},{9,11},{10,... | collective-permute-start | bytes 491528 | tf_op jit(solution)/shard_map/ppermute | solution.py:44
  181.6 2.7 %collective-permute-done.58.x3 = bf16[16,40,128]{2,1,0:T(8,128)(2,1)} collective-permute-done((bf16[16,40,128]{2,1,0:T(8,128)(2,1)}, bf16[16,40,128]{2,1,0:T(8,128)(2,1)}, u32[]{:S(2)}, u32[]{:S(2)}) %collective-permute-start.58) | collective-permute-done | bytes 163872 | tf_op jit(solution)/shard_map/ppermute | solution.py:44
  185.3 2.2 %shard_map.186 = (f32[16,7168]{1,0:T(8,128)S(1)}, bf16[16,7168]{1,0:T(8,128)(2,1)S(1)}, bf16[16,7168]{1,0:T(8,128)(2,1)S(1)}, bf16[16,7168]{1,0:T(8,128)(2,1)S(1)}) custom-call(f32[32,7168]{1,0:T(8,128)S(1)} %shard_map.184.before, f32[2,96,32]{2,1,0:T(8,128)S(1)} %copy-done.20, bf16[24,3584]{1,0:T(8,128)(2,1)S(1)} %get-tuple-element.348.f0, ...), custom_call_target="tpu_custom_call" | custom-call | bytes 1630208 | tf_op jit(solution)/shard_map/pallas_call | solution.py:63
  187.4 2.4 %collective-permute-start.59 = (bf16[16,7168]{1,0:T(8,128)(2,1)S(1)}, bf16[16,7168]{1,0:T(8,128)(2,1)S(1)}, u32[]{:S(2)}, u32[]{:S(2)}) collective-permute-start(bf16[16,7168]{1,0:T(8,128)(2,1)S(1)} %get-tuple-element.353), channel_id=1, source_target_pairs={{0,48},{16,0},{32,16},{48,32},{1,49},{17,1},{33,17},{49,33},{2,50}... | collective-permute-start | bytes 688136 | tf_op jit(solution)/shard_map/ppermute | solution.py:44
  201.8 2.7 %shard_map.189 = (bf16[896,128]{1,0:T(8,128)(2,1)S(1)}, bf16[16,576]{1,0:T(8,128)(2,1)S(1)}) custom-call(s32[1]{0:T(128)} %bitcast.core, bf16[16,7168]{1,0:T(8,128)(2,1)S(1)} %get-tuple-element.189.hidden, f32[16,7168]{1,0:T(8,128)S(1)} %get-tuple-element.363.own, bf16[16,7168]{1,0:T(8,128)(2,1)S(1)} %collective-permute-done.59.a, ...), custom_call_target="tpu_custom_call" | custom-call | bytes 9672708 | tf_op jit(solution)/shard_map/pallas_call | solution.py:63
  205.2 5.8 %shard_map.190 = bf16[7,1024,128]{2,1,0:T(8,128)(2,1)} custom-call(bf16[2,7,576,128]{3,2,1,0:T(8,128)(2,1)S(1)} %bitcast.45, bf16[8,8,576]{2,1,0:T(8,128)(2,1)S(1)} %pad.14.new_keys, f32[6,2,128,512]{3,2,1,0:T(8,128)S(1)} %copy-done.9, f32[6,2,128,1]{3,2,1,0:T(8,128)S(1)} %copy-done.11, f32[6,2,128,1]{3,2,1,0:T(8,128)S(1)} %copy-done.13, ...), custom_call_target="tpu_custom_call" | custom-call | tf_op jit(solution)/shard_map/pallas_call | solution.py:400
  (209 shorter events, 86.8 us)
Async XLA Ops:
  2.6 12.2 %collective-permute-start.3 = (bf16[16,40,128]{2,1,0:T(8,128)(2,1)S(1)}, bf16[16,40,128]{2,1,0:T(8,128)(2,1)S(1)}, u32[]{:S(2)}, u32[]{:S(2)}) collective-permute-start(bf16[16,40,128]{2,1,0:T(8,128)(2,1)S(1)} %get-tuple-element.192), channel_id=1, source_target_pairs={{0,1},{1,2},{2,3},{3,0},{4,5},{5,6},{6,7},{7,4},{8,9},{9,10},{10,1... | collective-permute-start | bytes 491528 | tf_op jit(solution)/shard_map/ppermute | solution.py:44
  6.8 14.3 %collective-permute-start = (bf16[16,7296]{1,0:T(8,128)(2,1)S(1)}, bf16[16,7296]{1,0:T(8,128)(2,1)S(1)}, u32[]{:S(2)}, u32[]{:S(2)}) collective-permute-start(bf16[16,7296]{1,0:T(8,128)(2,1)S(1)} %get-tuple-element.195.b0), channel_id=1, source_target_pairs={{0,16},{16,32},{32,48},{48,0},{1,17},{17,33},{33,49},{49,1},{2,18}... | collective-permute-start | bytes 700424 | tf_op jit(solution)/shard_map/ppermute | solution.py:44
  8.5 12.7 %collective-permute-start.1 = (bf16[16,7296]{1,0:T(8,128)(2,1)S(1)}, bf16[16,7296]{1,0:T(8,128)(2,1)S(1)}, u32[]{:S(2)}, u32[]{:S(2)}) collective-permute-start(bf16[16,7296]{1,0:T(8,128)(2,1)S(1)} %get-tuple-element.195.b0), channel_id=1, source_target_pairs={{0,48},{16,0},{32,16},{48,32},{1,49},{17,1},{33,17},{49,33},{2,50}... | collective-permute-start | bytes 700424 | tf_op jit(solution)/shard_map/ppermute | solution.py:44
  10.1 11.4 %collective-permute-start.2 = (bf16[16,7296]{1,0:T(8,128)(2,1)S(1)}, bf16[16,7296]{1,0:T(8,128)(2,1)S(1)}, u32[]{:S(2)}, u32[]{:S(2)}) collective-permute-start(bf16[16,7296]{1,0:T(8,128)(2,1)S(1)} %get-tuple-element.195.b0), channel_id=1, source_target_pairs={{0,32},{16,48},{32,0},{48,16},{1,33},{17,49},{33,1},{49,17},{2,34}... | collective-permute-start | bytes 700424 | tf_op jit(solution)/shard_map/ppermute | solution.py:44
  21.5 11.8 %collective-permute-start.10 = (bf16[16,40,128]{2,1,0:T(8,128)(2,1)S(1)}, bf16[16,40,128]{2,1,0:T(8,128)(2,1)S(1)}, u32[]{:S(2)}, u32[]{:S(2)}) collective-permute-start(bf16[16,40,128]{2,1,0:T(8,128)(2,1)S(1)} %get-tuple-element.215), channel_id=1, source_target_pairs={{0,32},{16,48},{32,0},{48,16},{1,33},{17,49},{33,1},{49,17},{2,34}... | collective-permute-start | bytes 491528 | tf_op jit(solution)/shard_map/ppermute | solution.py:44
  24.3 15.6 %collective-permute-start.6 = (bf16[24,3584]{1,0:T(8,128)(2,1)S(1)}, bf16[24,3584]{1,0:T(8,128)(2,1)S(1)}, u32[]{:S(2)}, u32[]{:S(2)}) collective-permute-start(bf16[24,3584]{1,0:T(8,128)(2,1)S(1)} %get-tuple-element.200), channel_id=1, source_target_pairs={{0,4},{4,8},{8,12},{12,0},{1,5},{5,9},{9,13},{13,1},{2,6},{6,10},{... | collective-permute-start | bytes 516104 | tf_op jit(solution)/shard_map/ppermute | solution.py:44
  26.3 13.6 %collective-permute-start.7 = (bf16[24,3584]{1,0:T(8,128)(2,1)S(1)}, bf16[24,3584]{1,0:T(8,128)(2,1)S(1)}, u32[]{:S(2)}, u32[]{:S(2)}) collective-permute-start(bf16[24,3584]{1,0:T(8,128)(2,1)S(1)} %get-tuple-element.201), channel_id=1, source_target_pairs={{0,8},{4,12},{8,0},{12,4},{1,9},{5,13},{9,1},{13,5},{2,10},{6,14},... | collective-permute-start | bytes 516104 | tf_op jit(solution)/shard_map/ppermute | solution.py:44
  40.7 14.6 %collective-permute-start.12 = (bf16[48,7168]{1,0:T(8,128)(2,1)S(1)}, bf16[48,7168]{1,0:T(8,128)(2,1)S(1)}, u32[]{:S(2)}, u32[]{:S(2)}) collective-permute-start(bf16[48,7168]{1,0:T(8,128)(2,1)S(1)} %shard_map.172), channel_id=1, source_target_pairs={{0,1},{1,2},{2,3},{3,0},{4,5},{5,6},{6,7},{7,4},{8,9},{9,10},{10,1... | collective-permute-start | bytes 2064392 | tf_op jit(solution)/shard_map/ppermute | solution.py:44
  42.3 13.4 %collective-permute-start.13 = (bf16[48,7168]{1,0:T(8,128)(2,1)S(1)}, bf16[48,7168]{1,0:T(8,128)(2,1)S(1)}, u32[]{:S(2)}, u32[]{:S(2)}) collective-permute-start(bf16[48,7168]{1,0:T(8,128)(2,1)S(1)} %shard_map.172), channel_id=1, source_target_pairs={{0,3},{1,0},{2,1},{3,2},{4,7},{5,4},{6,5},{7,6},{8,11},{9,8},{10,9... | collective-permute-start | bytes 2064392 | tf_op jit(solution)/shard_map/ppermute | solution.py:44
  55.9 11.9 %collective-permute-start.19 = (bf16[144,7168]{1,0:T(8,128)(2,1)S(1)}, bf16[144,7168]{1,0:T(8,128)(2,1)S(1)}, u32[]{:S(2)}, u32[]{:S(2)}) collective-permute-start(bf16[144,7168]{1,0:T(8,128)(2,1)S(1)} %constant_dynamic-update-slice_fusion.refs_0_), channel_id=1, source_target_pairs={{0,64},{64,0},{1,65},{65,1},{2,66},{66,2},{3,67},{67,3},{4,68},{68... | collective-permute-start | bytes 6193160 | tf_op jit(solution)/shard_map/ppermute | solution.py:44
  56.0 11.7 %collective-permute-start.17 = (bf16[24,7168]{1,0:T(8,128)(2,1)S(1)}, bf16[24,7168]{1,0:T(8,128)(2,1)S(1)}, u32[]{:S(2)}, u32[]{:S(2)}) collective-permute-start(bf16[24,7168]{1,0:T(8,128)(2,1)S(1)} %slice.33), channel_id=1, source_target_pairs={{0,1},{1,2},{2,3},{3,0},{4,5},{5,6},{6,7},{7,4},{8,9},{9,10},{10,1... | collective-permute-start | bytes 1032200 | tf_op jit(solution)/shard_map/ppermute | solution.py:44
  68.3 18.6 %collective-permute-start.20 = (bf16[48,7168]{1,0:T(8,128)(2,1)S(1)}, bf16[48,7168]{1,0:T(8,128)(2,1)S(1)}, u32[]{:S(2)}, u32[]{:S(2)}) collective-permute-start(bf16[48,7168]{1,0:T(8,128)(2,1)S(1)} %shard_map.174), channel_id=1, source_target_pairs={{0,1},{1,2},{2,3},{3,0},{4,5},{5,6},{6,7},{7,4},{8,9},{9,10},{10,1... | collective-permute-start | bytes 2064392 | tf_op jit(solution)/shard_map/ppermute | solution.py:44
  69.0 17.9 %collective-permute-start.21 = (bf16[48,7168]{1,0:T(8,128)(2,1)S(1)}, bf16[48,7168]{1,0:T(8,128)(2,1)S(1)}, u32[]{:S(2)}, u32[]{:S(2)}) collective-permute-start(bf16[48,7168]{1,0:T(8,128)(2,1)S(1)} %shard_map.174), channel_id=1, source_target_pairs={{0,3},{1,0},{2,1},{3,2},{4,7},{5,4},{6,5},{7,6},{8,11},{9,8},{10,9... | collective-permute-start | bytes 2064392 | tf_op jit(solution)/shard_map/ppermute | solution.py:44
  71.5 13.0 %collective-permute-start.24 = (bf16[16,40,128]{2,1,0:T(8,128)(2,1)S(1)}, bf16[16,40,128]{2,1,0:T(8,128)(2,1)S(1)}, u32[]{:S(2)}, u32[]{:S(2)}) collective-permute-start(bf16[16,40,128]{2,1,0:T(8,128)(2,1)S(1)} %get-tuple-element.252), channel_id=1, source_target_pairs={{0,4},{4,8},{8,12},{12,0},{1,5},{5,9},{9,13},{13,1},{2,6},{6,10},{... | collective-permute-start | bytes 491528 | tf_op jit(solution)/shard_map/ppermute | solution.py:44
  73.0 11.4 %collective-permute-start.25 = (bf16[16,40,128]{2,1,0:T(8,128)(2,1)S(1)}, bf16[16,40,128]{2,1,0:T(8,128)(2,1)S(1)}, u32[]{:S(2)}, u32[]{:S(2)}) collective-permute-start(bf16[16,40,128]{2,1,0:T(8,128)(2,1)S(1)} %get-tuple-element.253), channel_id=1, source_target_pairs={{0,8},{4,12},{8,0},{12,4},{1,9},{5,13},{9,1},{13,5},{2,10},{6,14},... | collective-permute-start | bytes 491528 | tf_op jit(solution)/shard_map/ppermute | solution.py:44
  87.1 12.6 %collective-permute-start.29 = (bf16[144,7168]{1,0:T(8,128)(2,1)S(1)}, bf16[144,7168]{1,0:T(8,128)(2,1)S(1)}, u32[]{:S(2)}, u32[]{:S(2)}) collective-permute-start(bf16[144,7168]{1,0:T(8,128)(2,1)S(1)} %constant_dynamic-update-slice_fusion.3.refs_0_), channel_id=1, source_target_pairs={{0,64},{64,0},{1,65},{65,1},{2,66},{66,2},{3,67},{67,3},{4,68},{68... | collective-permute-start | bytes 6193160 | tf_op jit(solution)/shard_map/ppermute | solution.py:44
  87.8 11.9 %collective-permute-start.31 = (bf16[64,40,128]{2,1,0:T(8,128)(2,1)S(1)}, bf16[64,40,128]{2,1,0:T(8,128)(2,1)S(1)}, u32[]{:S(2)}, u32[]{:S(2)}) collective-permute-start(bf16[64,40,128]{2,1,0:T(8,128)(2,1)S(1)} %constant_dynamic-update-slice_fusion.6.here), channel_id=1, source_target_pairs={{0,64},{64,0},{1,65},{65,1},{2,66},{66,2},{3,67},{67,3},{4,68},{68... | collective-permute-start | bytes 1966088 | tf_op jit(solution)/shard_map/ppermute | solution.py:44
  88.0 11.7 %collective-permute-start.27 = (bf16[24,7168]{1,0:T(8,128)(2,1)S(1)}, bf16[24,7168]{1,0:T(8,128)(2,1)S(1)}, u32[]{:S(2)}, u32[]{:S(2)}) collective-permute-start(bf16[24,7168]{1,0:T(8,128)(2,1)S(1)} %slice.35), channel_id=1, source_target_pairs={{0,1},{1,2},{2,3},{3,0},{4,5},{5,6},{6,7},{7,4},{8,9},{9,10},{10,1... | collective-permute-start | bytes 1032200 | tf_op jit(solution)/shard_map/ppermute | solution.py:44
  100.3 18.6 %collective-permute-start.32 = (bf16[48,7168]{1,0:T(8,128)(2,1)S(1)}, bf16[48,7168]{1,0:T(8,128)(2,1)S(1)}, u32[]{:S(2)}, u32[]{:S(2)}) collective-permute-start(bf16[48,7168]{1,0:T(8,128)(2,1)S(1)} %get-tuple-element.270), channel_id=1, source_target_pairs={{0,1},{1,2},{2,3},{3,0},{4,5},{5,6},{6,7},{7,4},{8,9},{9,10},{10,1... | collective-permute-start | bytes 2064392 | tf_op jit(solution)/shard_map/ppermute | solution.py:44
  101.5 17.4 %collective-permute-start.33 = (bf16[48,7168]{1,0:T(8,128)(2,1)S(1)}, bf16[48,7168]{1,0:T(8,128)(2,1)S(1)}, u32[]{:S(2)}, u32[]{:S(2)}) collective-permute-start(bf16[48,7168]{1,0:T(8,128)(2,1)S(1)} %get-tuple-element.271), channel_id=1, source_target_pairs={{0,3},{1,0},{2,1},{3,2},{4,7},{5,4},{6,5},{7,6},{8,11},{9,8},{10,9... | collective-permute-start | bytes 2064392 | tf_op jit(solution)/shard_map/ppermute | solution.py:44
  103.5 42.3 %collective-permute-start.47 = (bf16[576,3584]{1,0:T(8,128)(2,1)S(1)}, bf16[576,3584]{1,0:T(8,128)(2,1)S(1)}, u32[]{:S(2)}, u32[]{:S(2)}) collective-permute-start(bf16[576,3584]{1,0:T(8,128)(2,1)S(1)} %bitcast.46), channel_id=1, source_target_pairs={{0,64},{64,0},{1,65},{65,1},{2,66},{66,2},{3,67},{67,3},{4,68},{68... | collective-permute-start | bytes 12386312 | tf_op jit(solution)/shard_map/ppermute | solution.py:44
  120.5 17.2 %collective-permute-start.38 = (bf16[192,7168]{1,0:T(8,128)(2,1)S(1)}, bf16[192,7168]{1,0:T(8,128)(2,1)S(1)}, u32[]{:S(2)}, u32[]{:S(2)}) collective-permute-start(bf16[192,7168]{1,0:T(8,128)(2,1)S(1)} %get-tuple-element.288), channel_id=1, source_target_pairs={{0,64},{64,0},{1,65},{65,1},{2,66},{66,2},{3,67},{67,3},{4,68},{68... | collective-permute-start | bytes 8257544 | tf_op jit(solution)/shard_map/ppermute | solution.py:44
  120.6 18.5 %collective-permute-start.37 = (bf16[24,7168]{1,0:T(8,128)(2,1)S(1)}, bf16[24,7168]{1,0:T(8,128)(2,1)S(1)}, u32[]{:S(2)}, u32[]{:S(2)}) collective-permute-start(bf16[24,7168]{1,0:T(8,128)(2,1)S(1)} %add_convert_fusion.2), channel_id=1, source_target_pairs={{0,3},{1,0},{2,1},{3,2},{4,7},{5,4},{6,5},{7,6},{8,11},{9,8},{10,9... | collective-permute-start | bytes 1032200 | tf_op jit(solution)/shard_map/ppermute | solution.py:44
  123.7 15.4 %collective-permute-start.36 = (bf16[24,7168]{1,0:T(8,128)(2,1)S(1)}, bf16[24,7168]{1,0:T(8,128)(2,1)S(1)}, u32[]{:S(2)}, u32[]{:S(2)}) collective-permute-start(bf16[24,7168]{1,0:T(8,128)(2,1)S(1)} %add_convert_fusion.3), channel_id=1, source_target_pairs={{0,1},{1,2},{2,3},{3,0},{4,5},{5,6},{6,7},{7,4},{8,9},{9,10},{10,1... | collective-permute-start | bytes 1032200 | tf_op jit(solution)/shard_map/ppermute | solution.py:44
  139.1 15.4 %collective-permute-start.42 = (bf16[48,7168]{1,0:T(8,128)(2,1)S(1)}, bf16[48,7168]{1,0:T(8,128)(2,1)S(1)}, u32[]{:S(2)}, u32[]{:S(2)}) collective-permute-start(bf16[48,7168]{1,0:T(8,128)(2,1)S(1)} %get-tuple-element.303), channel_id=1, source_target_pairs={{0,1},{1,2},{2,3},{3,0},{4,5},{5,6},{6,7},{7,4},{8,9},{9,10},{10,1... | collective-permute-start | bytes 2064392 | tf_op jit(solution)/shard_map/ppermute | solution.py:44
  140.5 14.1 %collective-permute-start.43 = (bf16[48,7168]{1,0:T(8,128)(2,1)S(1)}, bf16[48,7168]{1,0:T(8,128)(2,1)S(1)}, u32[]{:S(2)}, u32[]{:S(2)}) collective-permute-start(bf16[48,7168]{1,0:T(8,128)(2,1)S(1)} %get-tuple-element.304), channel_id=1, source_target_pairs={{0,3},{1,0},{2,1},{3,2},{4,7},{5,4},{6,5},{7,6},{8,11},{9,8},{10,9... | collective-permute-start | bytes 2064392 | tf_op jit(solution)/shard_map/ppermute | solution.py:44
  143.2 11.3 %collective-permute-start.44 = (bf16[24,3584]{1,0:T(8,128)(2,1)S(1)}, bf16[24,3584]{1,0:T(8,128)(2,1)S(1)}, u32[]{:S(2)}, u32[]{:S(2)}) collective-permute-start(bf16[24,3584]{1,0:T(8,128)(2,1)S(1)} %get-tuple-element.309), channel_id=1, source_target_pairs={{0,12},{4,0},{8,4},{12,8},{1,13},{5,1},{9,5},{13,9},{2,14},{6,2},{... | collective-permute-start | bytes 516104 | tf_op jit(solution)/shard_map/ppermute | solution.py:44
  154.6 13.6 %collective-permute-start.49 = (bf16[24,7168]{1,0:T(8,128)(2,1)S(1)}, bf16[24,7168]{1,0:T(8,128)(2,1)S(1)}, u32[]{:S(2)}, u32[]{:S(2)}) collective-permute-start(bf16[24,7168]{1,0:T(8,128)(2,1)S(1)} %add_convert_fusion), channel_id=1, source_target_pairs={{0,3},{1,0},{2,1},{3,2},{4,7},{5,4},{6,5},{7,6},{8,11},{9,8},{10,9... | collective-permute-start | bytes 1032200 | tf_op jit(solution)/shard_map/ppermute | solution.py:44
  171.0 13.4 %collective-permute-start.53 = (bf16[24,3584]{1,0:T(8,128)(2,1)}, bf16[24,3584]{1,0:T(8,128)(2,1)S(1)}, u32[]{:S(2)}, u32[]{:S(2)}) collective-permute-start(bf16[24,3584]{1,0:T(8,128)(2,1)} %get-tuple-element.341), channel_id=1, source_target_pairs={{0,12},{4,0},{8,4},{12,8},{1,13},{5,1},{9,5},{13,9},{2,14},{6,2},{... | collective-permute-start | bytes 516104 | tf_op jit(solution)/shard_map/ppermute | solution.py:44
  173.1 11.3 %collective-permute-start.54 = (bf16[24,3584]{1,0:T(8,128)(2,1)}, bf16[24,3584]{1,0:T(8,128)(2,1)}, u32[]{:S(2)}, u32[]{:S(2)}) collective-permute-start(bf16[24,3584]{1,0:T(8,128)(2,1)} %get-tuple-element.342), channel_id=1, source_target_pairs={{0,8},{4,12},{8,0},{12,4},{1,9},{5,13},{9,1},{13,5},{2,10},{6,14},... | collective-permute-start | bytes 516104 | tf_op jit(solution)/shard_map/ppermute | solution.py:44
  173.1 11.3 %collective-permute-start.55 = (bf16[24,3584]{1,0:T(8,128)(2,1)}, bf16[24,3584]{1,0:T(8,128)(2,1)}, u32[]{:S(2)}, u32[]{:S(2)}) collective-permute-start(bf16[24,3584]{1,0:T(8,128)(2,1)} %get-tuple-element.343), channel_id=1, source_target_pairs={{0,4},{4,8},{8,12},{12,0},{1,5},{5,9},{9,13},{13,1},{2,6},{6,10},{... | collective-permute-start | bytes 516104 | tf_op jit(solution)/shard_map/ppermute | solution.py:44
  187.4 11.6 %collective-permute-start.59 = (bf16[16,7168]{1,0:T(8,128)(2,1)S(1)}, bf16[16,7168]{1,0:T(8,128)(2,1)S(1)}, u32[]{:S(2)}, u32[]{:S(2)}) collective-permute-start(bf16[16,7168]{1,0:T(8,128)(2,1)S(1)} %get-tuple-element.353), channel_id=1, source_target_pairs={{0,48},{16,0},{32,16},{48,32},{1,49},{17,1},{33,17},{49,33},{2,50}... | collective-permute-start | bytes 688136 | tf_op jit(solution)/shard_map/ppermute | solution.py:44
  (61 other events, 561.3 us)
